TPU v7x, 128 devices: a whole 4x4x4 slice. The times are simulated.
128 devices in a mesh: dp: 4 (over y), slab: 32 (over z, x, core).
Axes of the slice: x: 4, y: 4, z: 4, core: 2. Of those that a mesh axis runs over, the one named last changes fastest.
Arguments:
- grad_out: bfloat16 [4, 32, 128, 128, 128], P('dp', None, 'slab'), may hold values from -6 to 6
- pre_act: bfloat16 [4, 32, 128, 128, 128], P('dp', None, 'slab'), may hold values from -9 to 9
- forward_modes: bfloat16 [4, 32, 2, 32, 512], P('dp', 'slab'), may hold values from -6 to 6
- spec_weight: bfloat16 [32, 2, 32, 32, 512], P('slab', None, None, 'dp'), may hold values from -18 to 18
- w_local: bfloat16 [32, 32], replicated, may hold values from -1 to 1
Outputs:
- grad_in: bfloat16 [4, 32, 128, 128, 128], P('dp', None, 'slab')
- spec_weight_grad: float32 [32, 2, 32, 32, 512], P('slab', None, None, 'dp')
All inputs are finite; a program needn't handle non-finite values.
Results may differ from a plain program's by a relative error of at most 0.014.
Values may be sent and summed in bfloat16 or wider, within the bound.
No kernel may reach another device: no remote copies, remote signals or barrier semaphores. Data moves between devices by JAX's collectives and lax.ppermute only.
A program may use at most 128 MiB of HBM per device.

v0:
```python
import math

import jax
import jax.numpy as jnp
import numpy as np
from jax import lax
from jax.sharding import PartitionSpec as P

KX = 32
KY = 32
KZ = 16
KH = 4
KL = 4
ALL = ("dp", "slab")
BF = jnp.bfloat16
F32 = jnp.float32


def kept(count, length):
    index = np.arange(count)
    return np.where(index < count // 2, index, length - count + index)


def angles(modes, length):
    return (modes[:, None] * np.arange(length)[None, :] % length) * (2.0 * math.pi / length)


def z_analysis(ny, nz):
    ang = angles(np.arange(KZ), nz)
    weight = np.where(np.arange(KZ) == 0, 1.0, 2.0)[:, None]
    scale = 1.0 / math.sqrt(ny * nz)
    real, imag = (np.cos(ang) * weight * scale).T, (-np.sin(ang) * weight * scale).T
    return real, imag


def x_table(nx):
    ang = angles(kept(KX, nx), nx)
    scale = 1.0 / math.sqrt(nx)
    cos, sin = np.cos(ang) * scale, np.sin(ang) * scale
    out = np.zeros((nx, 2, 2, KX))
    out[:, 0, 0], out[:, 0, 1] = cos.T, -sin.T
    out[:, 1, 0], out[:, 1, 1] = sin.T, cos.T
    return out


def bf(table):
    return jnp.asarray(table, F32).astype(BF)


def gelu_slope(value):
    cdf = 0.5 * (1.0 + lax.erf(value * 0.7071067811865476))
    return cdf + value * jnp.exp(-0.5 * value * value) * 0.3989422804014327


def dot(spec, left, right):
    return jnp.einsum(spec, left, right, preferred_element_type=F32)


def shards(grad_out, pre_act, forward_modes, spec_weight, w_local):
    _, chans, planes, ny, nz = grad_out.shape
    dps, slabs = lax.axis_size("dp"), lax.axis_size("slab")
    nx = planes * slabs
    devs = dps * slabs
    share = chans // dps
    me = lax.axis_index("dp")

    vs = spec_weight.reshape(2, chans, share, devs, KL)
    vs = vs.transpose(3, 4, 0, 1, 2).reshape(devs, 16, 128)
    vs = lax.all_to_all(vs, ALL, 0, 0, tiled=True)
    vs = vs.reshape(dps, slabs, KL, 2, chans, share).transpose(3, 4, 0, 5, 1, 2)
    vs = vs.reshape(2, chans, chans, slabs * KL).astype(F32)

    fm = forward_modes.reshape(2, chans, KY * KZ)
    fms = [fm]
    for hop in range(1, dps):
        fms.append(lax.ppermute(fm, "dp", [(i, i ^ hop) for i in range(dps)]))

    dpre = (grad_out.astype(F32) * gelu_slope(pre_act.astype(F32))).astype(BF)[0]
    zr, zi = z_analysis(ny, nz)
    za = bf(np.stack([np.concatenate([zr, zi], 1), np.concatenate([zi, -zr], 1)], 1).reshape(nz, -1))
    tz = dot("cpyz,zk->cpyk", dpre, za).astype(BF).reshape(chans, planes, ny, 2, 2 * KZ)
    ang = angles(kept(KY, ny), ny)
    cs = bf(np.stack([np.cos(ang).T, np.sin(ang).T], 1))
    proj = dot("cpyhk,yhq->cpqk", tz, cs).astype(BF)
    proj = proj.reshape(chans, planes, KY, 2, KH, KL).transpose(2, 4, 1, 3, 5, 0)
    proj = proj.reshape(devs, planes * 2, KL * chans)
    got = lax.all_to_all(proj, ALL, 0, 0, tiled=True)
    got = got.reshape(dps, slabs * planes * 2, KL, chans)
    wx = x_table(nx)
    grad = dot("bxlo,xrj->brojl", got, bf(wx.reshape(nx * 2, 2, KX)))
    grad = grad.reshape(dps, 2, chans, KX * KL)
    gr, gi = grad[:, 0], grad[:, 1]

    def mix(left, right):
        return jnp.sum(left[:, None] * right[None], 2)

    back_r = mix(gr, vs[0]) + mix(gi, vs[1])
    back_i = mix(gi, vs[0]) - mix(gr, vs[1])
    back = jnp.stack([back_r, back_i], 1).astype(BF).reshape(dps, 2, chans, KX, KL)
    wi = bf(wx.transpose(2, 3, 0, 1).reshape(2, KX, nx * 2))
    xp = dot("brijl,rjx->bxli", back, wi).astype(BF)
    xp = xp.reshape(devs, planes * 2, KL * chans)
    gt = grad.astype(BF).reshape(dps, 2, chans, KX, KL).transpose(3, 1, 4, 0, 2).reshape(1, KX, 8, 128)
    gt = jnp.broadcast_to(gt, (dps, KX, 8, 128)).reshape(devs, 8, 128)
    got = lax.all_to_all(jnp.concatenate([xp, gt], 1), ALL, 0, 0, tiled=True)

    local = dot("io,opyz->ipyz", w_local, dpre)

    xq = got[:, :8].reshape(KY, KH, planes, 2, KL, chans).transpose(5, 2, 0, 3, 1, 4)
    xq = xq.reshape(chans, planes, KY, 2 * KZ)
    uv = dot("cpqk,yhq->cpyhk", xq, cs).astype(BF).reshape(chans, planes, ny, 4 * KZ)
    zang = angles(np.arange(KZ), nz)
    scale = 1.0 / math.sqrt(ny * nz)
    cz, sz = np.cos(zang) * scale, np.sin(zang) * scale
    zs = bf(np.concatenate([cz, -sz, -sz, -cz], 0))
    grad_in = (dot("cpyk,kz->cpyz", uv, zs) + local).astype(BF)[None]

    gm = got[:, 8:].reshape(devs, 2, KL, dps, dps, share)
    gm = lax.dynamic_index_in_dim(gm, me, 4, keepdims=False)
    gm = gm.transpose(3, 1, 4, 0, 2).reshape(dps, 2, share, KY * KZ).astype(F32)
    wr, wi_ = 0.0, 0.0
    for hop in range(dps):
        g = lax.dynamic_index_in_dim(gm, me ^ hop, 0, keepdims=False)
        u = fms[hop].astype(F32)
        g_r, g_i, u_r, u_i = g[0][None], g[1][None], u[0][:, None], u[1][:, None]
        wr = wr + g_r * u_r + g_i * u_i
        wi_ = wi_ + g_i * u_r - g_r * u_i
    spec_grad = jnp.stack([wr, wi_], 0)[None]
    return (grad_in, spec_grad)


def solution(mesh):
    return jax.shard_map(
        shards,
        mesh=mesh,
        in_specs=(
            P("dp", None, "slab", None, None),
            P("dp", None, "slab", None, None),
            P("dp", "slab", None, None, None),
            P("slab", None, None, "dp", None),
            P(),
        ),
        out_specs=(P("dp", None, "slab", None, None), P("slab", None, None, "dp", None)),
        check_vma=False,
    )
```

profile of v0, /device:TPU:1, one launch (start us, length us, event | category | flops | bytes accessed | tf_op | source)
XLA Modules:
  0.0 134.2 jit_solution(18133485331148398742)
XLA Ops:
  0.7 3.8 %collective-permute-start.1 = (bf16[2,32,512]{2,1,0:T(8,128)(2,1)}, bf16[2,32,512]{2,1,0:T(8,128)(2,1)S(1)}, u32[]{:S(2)}, u32[]{:S(2)}) collective-permute-start(bf16[2,32,512]{2,1,0:T(8,128)(2,1)} %bitcast.149), channel_id=1, source_target_pairs={{0,64},{32,96},{64,0},{96,32},{1,65},{33,97},{65,1},{97,33},{2,66}... | collective-permute-start | bytes 196616 | tf_op jit(solution)/shard_map/ppermute | solution.py:76
  5.3 6.3 %fusion.12 = bf16[32,4,128,128]{3,2,1,0:T(8,128)(2,1)S(1)} fusion(bf16[1,32,4,128,128]{4,3,2,1,0:T(8,128)(2,1)} %param.11, bf16[1,32,4,128,128]{4,3,2,1,0:T(8,128)(2,1)} %param.10), kind=kLoop, calls=%fused_computation.17 | loop fusion | flops 25165824 | bytes 12582912 | tf_op jit(solution)/shard_map/squeeze | solution.py:78
  11.6 1.6 %convolution_convert_fusion.1 = bf16[32,4,128,64]{2,3,1,0:T(8,128)(2,1)S(1)} fusion(bf16[32,4,128,128]{3,2,1,0:T(8,128)(2,1)S(1)} %fusion.12, bf16[128,64,1,1]{0,1,3,2:T(8,128)(2,1)S(1)} %copy-done.10), kind=kOutput, calls=%fused_computation.24 | convolution fusion | flops 269484032 | bytes 6307840 | tf_op jit(solution)/shard_map/cpyz,zk->cpyk/dot_general | solution.py:56
  13.2 0.7 bitcast_convert_fusion
  13.9 2.6 %copy.72 = bf16[32,4,32,2,4,4]{0,5,3,1,4,2:T(4,128)(2,1)S(1)} copy(bf16[32,4,32,2,4,4]{2,5,4,3,1,0:T(4,128)(2,1)S(1)} %bitcast.139) | data formatting | bytes 524288 | tf_op jit(solution)/shard_map/reshape | solution.py:85
  16.5 1.2 reshape.220
  17.7 11.1 %all-to-all-start = ((bf16[128,8,128]{2,1,0:T(8,128)(2,1)}), bf16[128,8,128]{2,1,0:T(8,128)(2,1)S(1)}, u32[]{:S(2)}, u32[]{:S(2)}) async-start(bf16[128,8,128]{2,1,0:T(8,128)(2,1)} %reshape.220), calls=%async_computation | async-start | bytes 524288 | tf_op jit(solution)/shard_map/all_to_all | solution.py:87
  28.8 8.0 %fusion.10 = f32[4,128,128,32]{2,3,1,0:T(8,128)} fusion(bf16[32,4,128,128]{3,2,1,0:T(8,128)(2,1)} %copy-done.2, bf16[32,32]{1,0:T(8,128)(2,1)S(1)} %copy-done), kind=kOutput, calls=%fused_computation.15 | convolution fusion | flops 134217728 | bytes 12584960 | tf_op jit(solution)/shard_map/io,opyz->ipyz/dot_general | solution.py:56
  36.9 0.6 slice_bitcast_fusion.9
  37.5 1.8 %copy.76 = bf16[1,2,32,8,512]{2,3,4,1,0:T(8,128)(2,1)S(1)} copy(bf16[1,2,32,8,512]{4,3,2,1,0:T(8,128)(2,1)S(1)} %copy-done.4) | data formatting | bytes 1048576 | tf_op args[3]
  39.3 1.8 %copy.77 = bf16[128,4,2,32,8]{0,4,3,2,1:T(8,128)(2,1)S(1)} copy(bf16[128,4,2,32,8]{3,4,1,0,2:T(8,128)(2,1)S(1)} %bitcast.132) | data formatting | bytes 1048576 | tf_op jit(solution)/shard_map/transpose | solution.py:68
  41.1 1.2 copy.78
  42.4 9.8 %all-to-all-start.1 = ((bf16[128,16,128]{2,1,0:T(8,128)(2,1)}), bf16[128,16,128]{2,1,0:T(8,128)(2,1)S(1)}, u32[]{:S(2)}, u32[]{:S(2)}) async-start(bf16[128,16,128]{2,1,0:T(8,128)(2,1)} %copy.78), calls=%async_computation.1 | async-start | bytes 1048576 | tf_op jit(solution)/shard_map/all_to_all | solution.py:69
  52.1 0.4 reshape.221
  52.6 0.4 fusion.15
  53.1 0.4 copy.90
  54.2 11.7 %all-to-all-done.1 = bf16[128,16,128]{2,1,0:T(8,128)(2,1)S(1)} async-done(((bf16[128,16,128]{2,1,0:T(8,128)(2,1)}), bf16[128,16,128]{2,1,0:T(8,128)(2,1)S(1)}, u32[]{:S(2)}, u32[]{:S(2)}) %all-to-all-start.1) | async-done | bytes 524320 | tf_op jit(solution)/shard_map/all_to_all | solution.py:69
  65.9 0.4 copy.79
  66.3 3.2 %reshape.233 = f32[4,32,4,2,32,8]{1,0,5,4,3,2:T(4,128)} reshape(f32[128,16,128]{0,2,1:T(8,128)S(1)} %copy.79) | data formatting | bytes 2097152 | tf_op jit(solution)/shard_map/convert_element_type | solution.py:71
  69.5 5.2 %fusion.22 = (f32[1,32,4,8,32,4]{4,2,3,1,0,5:T(4,128)}, f32[1,32,4,8,32,4]{4,2,3,1,0,5:T(4,128)}) fusion(f32[2,32,4,8,32,4]{4,2,3,1,0,5:T(4,128)} %bitcast.130), kind=kLoop, calls=%fused_computation.62 | loop fusion | bytes 2097152 | tf_op jit(solution)/shard_map/slice | solution.py:97
  74.7 3.2 %copy.83 = f32[1,32,4,8,32,4]{1,3,2,5,4,0:T(8,128)S(1)} copy(f32[1,32,4,8,32,4]{4,2,3,1,0,5:T(4,128)} %get-tuple-element.8) | data formatting | bytes 1048576 | tf_op jit(solution)/shard_map/slice | solution.py:97
  78.0 1.4 %copy.84 = f32[32,32,128]{2,1,0:T(8,128)S(1)} copy(f32[32,32,128]{0,1,2:T(8,128)S(1)} %bitcast.133) | data formatting | bytes 1048576 | tf_op jit(solution)/shard_map/mul | solution.py:95
  79.4 3.2 %copy.80 = f32[1,32,4,8,32,4]{1,3,2,5,4,0:T(8,128)S(1)} copy(f32[1,32,4,8,32,4]{4,2,3,1,0,5:T(4,128)} %get-tuple-element.9) | data formatting | bytes 1048576 | tf_op jit(solution)/shard_map/slice | solution.py:97
  82.7 1.4 %copy.81 = f32[32,32,128]{2,1,0:T(8,128)S(1)} copy(f32[32,32,128]{0,1,2:T(8,128)S(1)} %bitcast.134) | data formatting | bytes 1048576 | tf_op jit(solution)/shard_map/mul | solution.py:95
  84.1 1.7 %multiply_reduce_fusion.3 = (f32[4,32,128]{2,1,0:T(8,128)S(1)}, f32[4,32,128]{2,1,0:T(8,128)S(1)}, f32[4,32,128]{2,1,0:T(8,128)S(1)}, f32[4,32,128]{2,1,0:T(8,128)S(1)}) fusion(f32[32,32,128]{2,1,0:T(8,128)S(1)} %copy.81, f32[4,32,128]{2,1,0:T(8,128)S(1)} %copy.75, f32[4,32,128]{2,1,0:T(8,128)S(1)} %copy.82, f32[32,32,128]{2,1,0:T(8,128)S(1)} %copy.84), kind=kLoop, calls=%fused_computation.22 | loop fusion | flops 4128768 | bytes 1441792 | tf_op jit(solution)/shard_map/reduce_sum | solution.py:95
  86.4 1.0 fusion.14
  87.4 0.6 copy.89
  88.1 0.5 reshape.225
  88.6 0.9 pad_maximum_fusion
  89.5 4.5 %all-to-all-start.2 = ((bf16[128,16,128]{2,1,0:T(8,128)(2,1)}), bf16[128,16,128]{2,1,0:T(8,128)(2,1)S(1)}, u32[]{:S(2)}, u32[]{:S(2)}) async-start(bf16[128,16,128]{2,1,0:T(8,128)(2,1)} %pad_maximum_fusion), calls=%async_computation.2 | async-start | bytes 1048576 | tf_op jit(solution)/shard_map/all_to_all | solution.py:105
  94.0 0.7 slice_bitcast_fusion.5
  94.7 0.8 convert_element_type.118
  95.6 0.9 convert_element_type.120
  96.4 0.7 slice_bitcast_fusion.7
  97.1 0.7 slice_bitcast_fusion.3
  97.7 10.0 %all-to-all-done.2 = bf16[128,16,128]{2,1,0:T(8,128)(2,1)S(1)} async-done(((bf16[128,16,128]{2,1,0:T(8,128)(2,1)}), bf16[128,16,128]{2,1,0:T(8,128)(2,1)S(1)}, u32[]{:S(2)}, u32[]{:S(2)}) %all-to-all-start.2) | async-done | bytes 524320 | tf_op jit(solution)/shard_map/all_to_all | solution.py:105
  108.0 0.4 reshape.227
  108.4 2.4 %copy.91 = bf16[32,4,32,2,4,4]{2,5,4,3,1,0:T(4,128)(2,1)S(1)} copy(bf16[32,4,32,2,4,4]{0,5,3,1,4,2:T(4,128)(2,1)S(1)} %bitcast.142) | data formatting | bytes 524288 | tf_op jit(solution)/shard_map/transpose | solution.py:109
  110.9 2.0 %convolution_convert_fusion = bf16[32,4,32,128,2]{3,2,4,1,0:T(8,128)(2,1)} fusion(bf16[32,4,32,32,1]{2,3,4,1,0:T(8,128)(2,1)S(1)} %bitcast.138, bf16[128,2,32,1,1]{0,2,1,4,3:T(8,128)(2,1)S(1)} %copy-done.7), kind=kOutput, calls=%fused_computation.23 | convolution fusion | flops 68157440 | bytes 2375680 | tf_op jit(solution)/shard_map/cpqk,yhq->cpyhk/dot_general | solution.py:56
  112.9 0.9 copy.95
  113.8 0.9 dynamic-slice_bitcast_fusion.7
  114.7 1.8 %copy.96 = f32[8,512]{1,0:T(8,128)} copy(f32[8,512]{0,1:T(8,128)} %get-tuple-element.10) | data formatting | bytes 32768 | tf_op jit(solution)/shard_map/mul | solution.py:126
  116.5 1.7 %copy.102 = f32[8,512]{1,0:T(8,128)} copy(f32[8,512]{0,1:T(8,128)} %get-tuple-element.11) | data formatting | bytes 32768 | tf_op jit(solution)/shard_map/mul | solution.py:126
  118.2 1.6 %copy.100 = f32[8,512]{1,0:T(8,128)} copy(f32[8,512]{0,1:T(8,128)} %get-tuple-element.12) | data formatting | bytes 32768 | tf_op jit(solution)/shard_map/mul | solution.py:126
  119.8 0.7 copy.98
  120.9 1.6 %multiply_add_fusion = (f32[1,32,8,512]{3,2,1,0:T(8,128)S(1)}, f32[1,32,8,512]{3,2,1,0:T(8,128)S(1)}) fusion(f32[32,512]{1,0:T(8,128)} %get-tuple-element.31, f32[8,512]{1,0:T(8,128)S(1)} %copy.103, f32[32,512]{1,0:T(8,128)} %get-tuple-element.30, f32[8,512]{1,0:T(8,128)} %copy.102, f32[32,512]{1,0:T(8,128)} %get-tuple-element.29, f32[8,512]{1,0:T(8,128)S(1)} %copy.101, ...), kind=kLoop, calls=%fused_computation.33 | loop fusion | flops 3932160 | bytes 1703936 | tf_op jit(solution)/shard_map/add | solution.py:126
  122.6 1.0 maximum_bitcast_fusion
  123.6 10.6 %fusion.9 = bf16[1,32,4,128,128]{4,3,2,1,0:T(8,128)(2,1)} fusion(f32[4,128,128,32]{2,3,1,0:T(8,128)} %fusion.10, bf16[32,4,128,64]{2,3,1,0:T(8,128)(2,1)S(1)} %bitcast.136, bf16[64,128,1,1]{1,0,3,2:T(8,128)(2,1)} %constant.68), kind=kOutput, calls=%fused_computation.14 | convolution fusion | flops 272629760 | bytes 14696448 | tf_op jit(solution)/shard_map/cpyk,kz->cpyz/dot_general | solution.py:56
  (49 shorter events, 2.8 us)
Async XLA Ops:
  0.6 28.1 %copy-start = (bf16[32,32]{1,0:T(8,128)(2,1)S(1)}, bf16[32,32]{1,0:T(8,128)(2,1)}, u32[]{:S(2)}) copy-start(bf16[32,32]{1,0:T(8,128)(2,1)} %param.14) | copy-start | bytes 6148
  0.6 10.9 %copy-start.10 = (bf16[128,64,1,1]{0,1,3,2:T(8,128)(2,1)S(1)}, bf16[128,64,1,1]{0,1,3,2:T(8,128)(2,1)}, u32[]{:S(2)}) copy-start(bf16[128,64,1,1]{0,1,3,2:T(8,128)(2,1)} %constant.64) | copy-start | bytes 49156
  0.7 41.7 %collective-permute-start.1 = (bf16[2,32,512]{2,1,0:T(8,128)(2,1)}, bf16[2,32,512]{2,1,0:T(8,128)(2,1)S(1)}, u32[]{:S(2)}, u32[]{:S(2)}) collective-permute-start(bf16[2,32,512]{2,1,0:T(8,128)(2,1)} %bitcast.149), channel_id=1, source_target_pairs={{0,64},{32,96},{64,0},{96,32},{1,65},{33,97},{65,1},{97,33},{2,66}... | collective-permute-start | bytes 196616 | tf_op jit(solution)/shard_map/ppermute | solution.py:76
  4.5 90.2 %collective-permute-start = (bf16[2,32,512]{2,1,0:T(8,128)(2,1)}, bf16[2,32,512]{2,1,0:T(8,128)(2,1)}, u32[]{:S(2)}, u32[]{:S(2)}) collective-permute-start(bf16[2,32,512]{2,1,0:T(8,128)(2,1)} %bitcast.150), channel_id=1, source_target_pairs={{0,32},{32,0},{64,96},{96,64},{1,33},{33,1},{65,97},{97,65},{2,34}... | collective-permute-start | bytes 196616 | tf_op jit(solution)/shard_map/ppermute | solution.py:76
  4.9 90.7 %collective-permute-start.2 = (bf16[2,32,512]{2,1,0:T(8,128)(2,1)}, bf16[2,32,512]{2,1,0:T(8,128)(2,1)}, u32[]{:S(2)}, u32[]{:S(2)}) collective-permute-start(bf16[2,32,512]{2,1,0:T(8,128)(2,1)} %bitcast.151), channel_id=1, source_target_pairs={{0,96},{32,64},{64,32},{96,0},{1,97},{33,65},{65,33},{97,1},{2,98}... | collective-permute-start | bytes 196616 | tf_op jit(solution)/shard_map/ppermute | solution.py:76
  11.6 2.3 %copy-start.2 = (bf16[32,4,128,128]{3,2,1,0:T(8,128)(2,1)}, bf16[32,4,128,128]{3,2,1,0:T(8,128)(2,1)S(1)}, u32[]{:S(2)}) copy-start(bf16[32,4,128,128]{3,2,1,0:T(8,128)(2,1)S(1)} %fusion.12) | copy-start | bytes 12582916
  11.6 1.6 %copy-start.6 = (bf16[128,2,32,1,1]{0,2,1,4,3:T(8,128)(2,1)S(1)}, bf16[128,2,32,1,1]{0,2,1,4,3:T(8,128)(2,1)}, u32[]{:S(2)}) copy-start(bf16[128,2,32,1,1]{0,2,1,4,3:T(8,128)(2,1)} %constant.65) | copy-start | bytes 49156
  17.7 24.6 %all-to-all-start = ((bf16[128,8,128]{2,1,0:T(8,128)(2,1)}), bf16[128,8,128]{2,1,0:T(8,128)(2,1)S(1)}, u32[]{:S(2)}, u32[]{:S(2)}) async-start(bf16[128,8,128]{2,1,0:T(8,128)(2,1)} %reshape.220), calls=%async_computation | async-start | bytes 524288 | tf_op jit(solution)/shard_map/all_to_all | solution.py:87
  28.8 8.1 %copy-start.8 = (bf16[1,1,2,32,512]{4,3,2,1,0:T(8,128)(2,1)S(1)}, bf16[1,1,2,32,512]{4,3,2,1,0:T(8,128)(2,1)}, u32[]{:S(2)}) copy-start(bf16[1,1,2,32,512]{4,3,2,1,0:T(8,128)(2,1)} %param.12) | copy-start | bytes 196612
  28.8 8.7 %copy-start.4 = (bf16[1,2,32,8,512]{4,3,2,1,0:T(8,128)(2,1)S(1)}, bf16[1,2,32,8,512]{4,3,2,1,0:T(8,128)(2,1)}, u32[]{:S(2)}) copy-start(bf16[1,2,32,8,512]{4,3,2,1,0:T(8,128)(2,1)} %param.13) | copy-start | bytes 1572868
  37.5 15.1 %copy-start.9 = (bf16[256,2,32,1,1]{0,2,1,4,3:T(8,128)(2,1)S(1)}, bf16[256,2,32,1,1]{0,2,1,4,3:T(8,128)(2,1)}, u32[]{:S(2)}) copy-start(bf16[256,2,32,1,1]{0,2,1,4,3:T(8,128)(2,1)} %constant.66) | copy-start | bytes 98308
  42.4 23.5 %all-to-all-start.1 = ((bf16[128,16,128]{2,1,0:T(8,128)(2,1)}), bf16[128,16,128]{2,1,0:T(8,128)(2,1)S(1)}, u32[]{:S(2)}, u32[]{:S(2)}) async-start(bf16[128,16,128]{2,1,0:T(8,128)(2,1)} %copy.78), calls=%async_computation.1 | async-start | bytes 1048576 | tf_op jit(solution)/shard_map/all_to_all | solution.py:69
  88.6 22.3 %copy-start.7 = (bf16[128,2,32,1,1]{0,2,1,4,3:T(8,128)(2,1)S(1)}, bf16[128,2,32,1,1]{0,2,1,4,3:T(8,128)(2,1)}, u32[]{:S(2)}) copy-start(bf16[128,2,32,1,1]{0,2,1,4,3:T(8,128)(2,1)} %constant.65) | copy-start | bytes 49156
  89.5 18.2 %all-to-all-start.2 = ((bf16[128,16,128]{2,1,0:T(8,128)(2,1)}), bf16[128,16,128]{2,1,0:T(8,128)(2,1)S(1)}, u32[]{:S(2)}, u32[]{:S(2)}) async-start(bf16[128,16,128]{2,1,0:T(8,128)(2,1)} %pad_maximum_fusion), calls=%async_computation.2 | async-start | bytes 1048576 | tf_op jit(solution)/shard_map/all_to_all | solution.py:105
  112.9 8.0 %copy-start.5 = (f32[32,512]{1,0:T(8,128)S(1)}, f32[32,512]{1,0:T(8,128)}, u32[]{:S(2)}) copy-start(f32[32,512]{1,0:T(8,128)} %get-tuple-element.25) | copy-start | bytes 196612
  114.7 8.9 %copy-start.3 = (bf16[32,4,32,128,2]{3,2,4,1,0:T(8,128)(2,1)S(1)}, bf16[32,4,32,128,2]{3,2,4,1,0:T(8,128)(2,1)}, u32[]{:S(2)}) copy-start(bf16[32,4,32,128,2]{3,2,4,1,0:T(8,128)(2,1)} %convolution_convert_fusion) | copy-start | bytes 6291460
  123.6 10.6 %copy-start.1 = (bf16[32,32]{1,0:T(8,128)(2,1)S(1)}, bf16[32,32]{1,0:T(8,128)(2,1)}, u32[]{:S(2)}) copy-start(bf16[32,32]{1,0:T(8,128)(2,1)} %param.14) | copy-start | bytes 6148
where the time goes:
time: 135 us; the launch traced here: 134 us
  local copies, waits for them, and re-layouts  43.8 us (32%)
  starting transfers between devices  30 us (22%)
  matrix products  24.4 us (18%)
  waiting for transfers between devices  21.7 us (16%)
  other arithmetic  13.3 us (10%)
    dot_general x7, matrix products, dot(): return jnp.einsum(spec, left, right, preferred_element_type=F32)  24.4 us
    slice x3, local copies, waits for them, and re-layouts, shards(): back_r = mix(gr, vs[0]) + mix(gi, vs[1])  11.7 us
    all_to_all x1, waiting for transfers between devices, shards(): vs = lax.all_to_all(vs, ALL, 0, 0, tiled=True)  11.7 us
    all_to_all x1, starting transfers between devices, shards(): got = lax.all_to_all(proj, ALL, 0, 0, tiled=True)  11.1 us
    all_to_all x1, waiting for transfers between devices, shards(): got = lax.all_to_all(jnp.concatenate([xp, gt], 1), ALL, 0, 0, tiled=True)  10 us
    all_to_all x1, starting transfers between devices, shards(): vs = lax.all_to_all(vs, ALL, 0, 0, tiled=True)  9.78 us
    mul x13, local copies, waits for them, and re-layouts, shards(): wr = wr + g_r * u_r + g_i * u_i  9.75 us
    squeeze x1, other arithmetic, shards(): (grad_out.astype(F32) * gelu_slope(pre_act.astype(F32))).astype(BF)[0]  6.3 us
  transfers between devices with their start and end apart: 6, of which 2 were waited for; matrix products, arithmetic and copies ran while one was open for 41% of the time, Pallas kernels for 0%

commit v1 on v0

v1 whole, which is shorter than its diff:
```python
import functools
import math

import jax
import jax.numpy as jnp
import numpy as np
from jax import lax
from jax.experimental import pallas as pl
from jax.experimental.pallas import tpu as pltpu
from jax.sharding import PartitionSpec as P

C = 32
NP = 4
NY = 128
NZ = 128
KX = 32
KY = 32
KZ = 16
NB = 4
NS = 32
QL = 4
SHARE = C // NB
DEVS = NB * NS
STEPS = 8
CB = C // STEPS
ALL = ("dp", "slab")
BF = jnp.bfloat16
F32 = jnp.float32
VMEM_LIMIT = 56 * 1024 * 1024


def kept(count, length):
    index = np.arange(count)
    return np.where(index < count // 2, index, length - count + index)


def angles(modes, length):
    return (modes[:, None] * np.arange(length)[None, :] % length) * (2.0 * math.pi / length)


def bf(table):
    return jnp.asarray(table, F32).astype(BF)


@functools.cache
def z_analysis():
    ang = angles(np.arange(KZ), NZ)
    weight = np.where(np.arange(KZ) == 0, 1.0, 2.0)[:, None] / math.sqrt(NY * NZ)
    real, imag = (np.cos(ang) * weight).T, (-np.sin(ang) * weight).T
    out = np.zeros((NP, NZ, 2, KZ, NP, 2), np.float32)
    for p in range(NP):
        out[p, :, 0, :, p, 0], out[p, :, 0, :, p, 1] = real, imag
        out[p, :, 1, :, p, 0], out[p, :, 1, :, p, 1] = imag, -real
    return out.reshape(NP * NZ, 2 * 128)


@functools.cache
def z_synthesis():
    ang = angles(np.arange(KZ), NZ)
    scale = 1.0 / math.sqrt(NY * NZ)
    cos, sin = np.cos(ang) * scale, np.sin(ang) * scale
    out = np.zeros((2, KZ, NP, 2, NP, NZ), np.float32)
    for p in range(NP):
        out[0, :, p, 0, p], out[0, :, p, 1, p] = cos, -sin
        out[1, :, p, 0, p], out[1, :, p, 1, p] = -sin, -cos
    return out.reshape(2 * 128, NP * NZ)


@functools.cache
def y_table():
    ang = angles(kept(KY, NY), NY)
    return np.concatenate([np.cos(ang), np.sin(ang)], 0).astype(np.float32)


@functools.cache
def x_table():
    nx = NS * NP
    ang = angles(kept(KX, nx), nx)
    cos, sin = np.cos(ang).T / math.sqrt(nx), np.sin(ang).T / math.sqrt(nx)
    out = np.zeros((nx, 2, 2, KX), np.float32)
    out[:, 0, 0], out[:, 0, 1], out[:, 1, 0], out[:, 1, 1] = cos, -sin, sin, cos
    return out


@functools.cache
def x_forward():
    out = np.zeros((QL, NS * NP, 2, 2, QL, KX), np.float32)
    for ql in range(QL):
        out[ql, :, :, :, ql] = x_table()
    return out.reshape(QL, 256, 256)


@functools.cache
def x_inverse():
    out = np.zeros((QL, 2, QL, KX, NS * NP, 2), np.float32)
    for ql in range(QL):
        out[ql, :, ql] = x_table().transpose(2, 3, 0, 1)
    return out.reshape(QL, 256, 256)


def dot(left, right):
    return jnp.dot(left, right, preferred_element_type=F32)


def gelu_slope(x):
    a = jnp.abs(x)
    t = pl.reciprocal(1.0 + (0.3275911 * math.sqrt(0.5)) * a, approx=True)
    poly = 0.5 * 1.061405429 * t + 0.5 * -1.453152027
    poly = poly * t + 0.5 * 1.421413741
    poly = poly * t + 0.5 * -0.284496736
    poly = poly * t + 0.5 * 0.254829592
    tail = jnp.exp2(x * x * (-0.5 * math.log2(math.e))) * (poly * t - 0.3989422804014327 * a)
    return jnp.where(x >= 0.0, 1.0 - tail, tail)


def analysis_kernel(go_ref, pa_ref, sw_ref, za_ref, cs_ref, dpre_ref, send_ref, proj_ref, rows_ref):
    step = pl.program_id(0)
    for c in range(CB):
        parts = []
        for p in range(NP):
            value = go_ref[0, c, p].astype(F32) * gelu_slope(pa_ref[0, c, p].astype(F32))
            parts.append(value.astype(BF))
            dpre_ref[c, p] = parts[-1]
        tz = dot(jnp.concatenate(parts[:2], 1), za_ref[:256])
        tz = (tz + dot(jnp.concatenate(parts[2:], 1), za_ref[256:])).astype(BF)
        both = dot(cs_ref[...], tz)
        proj_ref[pl.ds((step * CB + c) * KY, KY), :] = both[:KY, :128] + both[KY:, 128:]

    block = sw_ref[0, 0].astype(F32).reshape(128, 256)
    j = step // 2
    for h in range(2):
        turned = block[:, h * 128 : (h + 1) * 128].T
        for qh in range(2):
            first = ((step % 2) * 4 + h * 2 + qh) * KZ
            for ql in range(QL):
                at = (qh * QL + ql) * KZ
                rows_ref[pl.ds(first * 24 + 8 + j * 4 + ql, KZ, stride=24), :] = turned[at : at + KZ]

    @pl.when(step == STEPS - 1)
    def _():
        for qh in range(KY // QL):
            group = [proj_ref[pl.ds(qh * QL + ql, C, stride=KY), :] for ql in range(QL)]
            turned = jnp.concatenate(group, 0).T
            for kz in range(KZ):
                rows_ref[pl.ds((qh * KZ + kz) * 24, 8), :] = turned[kz * 8 : kz * 8 + 8]
        send_ref[...] = rows_ref[...].reshape(DEVS, 24, 128).astype(BF)


def analysis(grad_out, pre_act, spec_weight):
    whole = lambda *shape: pl.BlockSpec(shape, lambda n: (0,) * len(shape))
    return pl.pallas_call(
        analysis_kernel,
        grid=(STEPS,),
        in_specs=[
            pl.BlockSpec((1, CB, NP, NY, NZ), lambda n: (0, n, 0, 0, 0)),
            pl.BlockSpec((1, CB, NP, NY, NZ), lambda n: (0, n, 0, 0, 0)),
            pl.BlockSpec((1, 1, 16, SHARE, 256), lambda n: (0, n // 4, (n // 2) % 2, 0, n % 2)),
            whole(NP * NZ, 256),
            whole(2 * KY, NY),
        ],
        out_specs=[
            pl.BlockSpec((CB, NP, NY, NZ), lambda n: (n, 0, 0, 0)),
            whole(DEVS, 24, 128),
        ],
        out_shape=[
            jax.ShapeDtypeStruct((C, NP, NY, NZ), BF),
            jax.ShapeDtypeStruct((DEVS, 24, 128), BF),
        ],
        scratch_shapes=[pltpu.VMEM((C * KY, 128), F32), pltpu.VMEM((DEVS * 24, 128), F32)],
        compiler_params=pltpu.CompilerParams(vmem_limit_bytes=VMEM_LIMIT),
        name="analysis",
    )(grad_out, pre_act, spec_weight, bf(z_analysis()), bf(y_table()))


def mix_kernel(got_ref, wf_ref, wi_ref, send_ref, rows_ref, v_ref, out_ref, g_ref, back_ref):
    rows_ref[...] = got_ref[...].astype(F32).reshape(DEVS * 24, 128)
    for j in range(4):
        for og in range(NB):
            first = og * NS * 24 + 8 + j * 4
            group = [rows_ref[pl.ds(first + ql, KX, stride=24), :] for ql in range(QL)]
            at = (j * NB + og) * 128
            v_ref[at : at + 128, :] = jnp.concatenate(group, 0).T

    planes = []
    for b in range(NB):
        part = [rows_ref[pl.ds((b * NS + s) * 24, 8), :] for s in range(NS)]
        planes.append(jnp.concatenate(part, 0).T.astype(BF))
    grad = jnp.zeros((NB * C, 256), F32)
    for ql in range(QL):
        left = jnp.concatenate([planes[b][ql * C : (ql + 1) * C] for b in range(NB)], 0)
        grad = grad + dot(left, wf_ref[ql])
    g_ref[...] = grad

    turned = grad.T
    for r in range(2):
        for ql in range(QL):
            at = (r * QL + ql) * KX
            for og in range(NB):
                first = og * NS * 16 + 8 + r * QL + ql
                out_ref[pl.ds(first, KX, stride=16), :] = turned[at : at + KX]

    for ig in range(4):
        acc = [[jnp.zeros((8, 128), F32) for _ in range(2)] for _ in range(NB)]
        for o in range(C):
            at = (o // SHARE) * 128 + (ig % 2) * 64 + o % SHARE
            vr = v_ref[pl.ds((ig // 2) * 512 + at, 8, stride=SHARE), :]
            vi = v_ref[pl.ds((2 + ig // 2) * 512 + at, 8, stride=SHARE), :]
            for b in range(NB):
                gr = g_ref[pl.ds(b * C + o, 1), :128]
                gi = g_ref[pl.ds(b * C + o, 1), 128:]
                acc[b][0] = acc[b][0] + gr * vr + gi * vi
                acc[b][1] = acc[b][1] + gi * vr - gr * vi
        for b in range(NB):
            back_ref[b * C + ig * 8 : b * C + ig * 8 + 8, :] = jnp.concatenate(acc[b], 1)

    back = back_ref[...].astype(BF)
    outs = [dot(back, wi_ref[ql]) for ql in range(QL)]
    for b in range(NB):
        turned = jnp.concatenate([outs[ql][b * C : (b + 1) * C] for ql in range(QL)], 0).T
        for s in range(NS):
            out_ref[pl.ds((b * NS + s) * 16, 8), :] = turned[s * 8 : s * 8 + 8]
    send_ref[...] = out_ref[...].reshape(DEVS, 16, 128).astype(BF)


def mix(got):
    return pl.pallas_call(
        mix_kernel,
        out_shape=jax.ShapeDtypeStruct((DEVS, 16, 128), BF),
        scratch_shapes=[
            pltpu.VMEM((DEVS * 24, 128), F32),
            pltpu.VMEM((16 * 128, 128), F32),
            pltpu.VMEM((DEVS * 16, 128), F32),
            pltpu.VMEM((128, 256), F32),
            pltpu.VMEM((128, 256), F32),
        ],
        compiler_params=pltpu.CompilerParams(vmem_limit_bytes=VMEM_LIMIT),
        name="mix",
    )(got, bf(x_forward()), bf(x_inverse()))


def synthesis_kernel(me_ref, got_ref, local_ref, fm0, fm1, fm2, fm3, cs_ref, zs_ref, out_ref, spec_ref, rows_ref, x_ref, g_ref, u_ref):
    step = pl.program_id(0)
    me = me_ref[0]

    @pl.when(step == 0)
    def _():
        rows_ref[...] = got_ref[...].astype(F32).reshape(DEVS * 16, 128)
        for qh in range(KY // QL):
            group = [rows_ref[pl.ds((qh * KZ + kz) * 16, 8), :] for kz in range(KZ)]
            turned = jnp.concatenate(group, 0).T
            for ql in range(QL):
                x_ref[pl.ds(qh * QL + ql, C, stride=KY), :] = turned[ql * C : (ql + 1) * C]
        for r in range(2):
            for tile in range(4):
                group = []
                for q in range(2 * QL):
                    first = (tile * 2 + q // QL) * KZ * 16 + 8 + r * QL + q % QL
                    group.append(rows_ref[pl.ds(first, KZ, stride=16), :])
                g_ref[r, :, tile * 128 : (tile + 1) * 128] = jnp.concatenate(group, 0).T
        for hop, fm in enumerate((fm0, fm1, fm2, fm3)):
            u_ref[hop] = fm[...].astype(F32)

    for pair in range(CB // 2):
        first = (step * CB + pair * 2) * KY
        xs = jnp.concatenate([x_ref[pl.ds(first, KY), :], x_ref[pl.ds(first + KY, KY), :]], 1)
        uv = dot(cs_ref[...], xs.astype(BF)).astype(BF)
        for k in range(2):
            left = jnp.concatenate([uv[:NY, k * 128 : k * 128 + 128], uv[NY:, k * 128 : k * 128 + 128]], 1)
            full = dot(left, zs_ref[...])
            for p in range(NP):
                c = pair * 2 + k
                total = full[:, p * NZ : (p + 1) * NZ] + local_ref[c, p].astype(F32)
                out_ref[0, c, p] = total.astype(BF)

    for k in range(CB):
        i = step * CB + k
        wr, wi = jnp.zeros((SHARE, KY * KZ), F32), jnp.zeros((SHARE, KY * KZ), F32)
        for hop in range(NB):
            at = pl.multiple_of((me ^ hop) * C + me * SHARE, SHARE)
            gr, gi = g_ref[0, pl.ds(at, SHARE), :], g_ref[1, pl.ds(at, SHARE), :]
            ur, ui = u_ref[hop, 0, pl.ds(i, 1), :], u_ref[hop, 1, pl.ds(i, 1), :]
            wr = wr + gr * ur + gi * ui
            wi = wi + gi * ur - gr * ui
        spec_ref[0, 0, k] = wr
        spec_ref[0, 1, k] = wi


def synthesis(me, got, local, fms):
    whole = lambda *shape: pl.BlockSpec(shape, lambda n: (0,) * len(shape))
    table = y_table().reshape(2, KY, NY).transpose(0, 2, 1).reshape(2 * NY, KY)
    return pl.pallas_call(
        synthesis_kernel,
        grid=(STEPS,),
        in_specs=[
            pl.BlockSpec(memory_space=pltpu.SMEM),
            whole(DEVS, 16, 128),
            pl.BlockSpec((CB, NP, NY, NZ), lambda n: (n, 0, 0, 0)),
            *[whole(2, C, KY * KZ)] * NB,
            whole(2 * NY, KY),
            whole(256, NP * NZ),
        ],
        out_specs=[
            pl.BlockSpec((1, CB, NP, NY, NZ), lambda n: (0, n, 0, 0, 0)),
            pl.BlockSpec((1, 2, CB, SHARE, KY * KZ), lambda n: (0, 0, n, 0, 0)),
        ],
        out_shape=[
            jax.ShapeDtypeStruct((1, C, NP, NY, NZ), BF),
            jax.ShapeDtypeStruct((1, 2, C, SHARE, KY * KZ), F32),
        ],
        scratch_shapes=[
            pltpu.VMEM((DEVS * 16, 128), F32),
            pltpu.VMEM((C * KY, 128), F32),
            pltpu.VMEM((2, 128, KY * KZ), F32),
            pltpu.VMEM((NB, 2, C, KY * KZ), F32),
        ],
        compiler_params=pltpu.CompilerParams(vmem_limit_bytes=VMEM_LIMIT),
        name="synthesis",
    )(me, got, local, *fms, bf(table), bf(z_synthesis()))


def shards(grad_out, pre_act, forward_modes, spec_weight, w_local):
    me = lax.axis_index("dp")
    dpre, send = analysis(grad_out, pre_act, spec_weight)
    got = lax.all_to_all(send, ALL, 0, 0, tiled=True)
    fm = forward_modes.reshape(2, C, KY * KZ)
    fms = [fm] + [lax.ppermute(fm, "dp", [(b, b ^ hop) for b in range(NB)]) for hop in range(1, NB)]
    local = jnp.einsum("io,opyz->ipyz", w_local, dpre, preferred_element_type=F32).astype(BF)
    got = lax.all_to_all(mix(got), ALL, 0, 0, tiled=True)
    return synthesis(me.reshape(1), got, local, fms)


def solution(mesh):
    return jax.shard_map(
        shards,
        mesh=mesh,
        in_specs=(
            P("dp", None, "slab", None, None),
            P("dp", None, "slab", None, None),
            P("dp", "slab", None, None, None),
            P("slab", None, None, "dp", None),
            P(),
        ),
        out_specs=(P("dp", None, "slab", None, None), P("slab", None, None, "dp", None)),
        check_vma=False,
    )
```

time: 135 us -> 78.9 us (0.58)
  local copies, waits for them, and re-layouts: 43.8 us -> 6.6 us
  blocking collectives: 0 us -> 28.2 us
  Pallas kernels: 0 us -> 27.5 us
  starting transfers between devices: 30 us -> 7.83 us
  waiting for transfers between devices: 21.7 us -> 0.01 us
  matrix products: 24.4 us -> 6.93 us
  other arithmetic: 13.3 us -> 0 us
    all_to_all x0 -> x1, blocking collectives: none -> 28.2 us  [shards(): got = lax.all_to_all(send, ALL, 0, 0, tiled=True)]
    pallas_call x0 -> x3, Pallas kernels: none -> 27.5 us  [the longest x1 13.7 us: analysis(): pl.pallas_call(analysis_kernel, grid=(STEPS,), in_specs=[pl.BlockSpec((1,...]
    all_to_all x3 -> x1, waiting for transfers between devices: 21.7 us -> 0.01 us  [shards(): got = lax.all_to_all(mix(got), ALL, 0, 0, tiled=True)]
    all_to_all x3 -> x1, starting transfers between devices: 25.4 us -> 4.42 us  [shards(): got = lax.all_to_all(mix(got), ALL, 0, 0, tiled=True)]
    dot_general x7 -> x1, matrix products: 24.4 us -> 6.93 us  [shards(): jnp.einsum('io,opyz->ipyz', w_local, dpre, preferred_element_type=F32)]
    mul x18 -> x0, local copies, waits for them, and re-layouts: 12.8 us -> none  [the longest x13 9.75 us: shards(): wr = wr + g_r * u_r + g_i * u_i]
    slice x5 -> x0, local copies, waits for them, and re-layouts: 12 us -> none  [the longest x3 11.7 us: shards(): back_r = mix(gr, vs[0]) + mix(gi, vs[1])]
    reshape x6 -> x0, local copies, waits for them, and re-layouts: 6.33 us -> none  [the longest x1 2.58 us: shards(): proj.reshape(chans, planes, KY, 2, KH, KL).transpose(2, 4, 1, 3, 5, 0)]
  transfers between devices with their start and end apart: 6 -> 4, of which waited for: 2 -> 0; matrix products, arithmetic and copies ran while one was open for 41% -> 16% of each run, Pallas kernels for 0% -> 0%
where the time goes in v1:
time: 78.9 us; the launch traced here: 77.7 us
  blocking collectives  28.2 us (36%)
  Pallas kernels  27.5 us (35%)
  starting transfers between devices  7.83 us (10%)
  matrix products  6.93 us (9%)
  local copies, waits for them, and re-layouts  6.6 us (8%)
    all_to_all x1, blocking collectives, shards(): got = lax.all_to_all(send, ALL, 0, 0, tiled=True)  28.2 us
    pallas_call x1, Pallas kernels, analysis(): pl.pallas_call(analysis_kernel, grid=(STEPS,), in_specs=[pl.BlockSpec((1,...  13.7 us
    pallas_call x1, Pallas kernels, synthesis(): pl.pallas_call(synthesis_kernel, grid=(STEPS,), in_specs=[pl.BlockSpec(me...  9.83 us
    dot_general x1, matrix products, shards(): jnp.einsum('io,opyz->ipyz', w_local, dpre, preferred_element_type=F32)  6.93 us
    dot_general x1, local copies, waits for them, and re-layouts, shards(): jnp.einsum('io,opyz->ipyz', w_local, dpre, preferred_element_type=F32)  5.76 us
    all_to_all x1, starting transfers between devices, shards(): got = lax.all_to_all(mix(got), ALL, 0, 0, tiled=True)  4.42 us
    pallas_call x1, Pallas kernels, mix(): pl.pallas_call(mix_kernel, out_shape=jax.ShapeDtypeStruct((DEVS, 16, 128)...  3.95 us
    ppermute x3, starting transfers between devices, shards(): lax.ppermute(fm, 'dp', [(b, b ^ hop) for b in range(NB)])  3.41 us
  transfers between devices with their start and end apart: 4, of which 0 were waited for; matrix products, arithmetic and copies ran while one was open for 16% of the time, Pallas kernels for 0%

profile of v1, /device:TPU:1, one launch (start us, length us, event | category | flops | bytes accessed | tf_op | source)
XLA Modules:
  0.0 77.7 jit_solution(10631497235576874381)
XLA Ops:
  0.6 0.0 copy-start
  0.6 13.7 %analysis.1 = (bf16[32,4,128,128]{3,2,1,0:T(8,128)(2,1)}, bf16[128,24,128]{2,1,0:T(8,128)(2,1)}) custom-call(bf16[1,32,4,128,128]{4,3,2,1,0:T(8,128)(2,1)} %go_ref.1, bf16[1,32,4,128,128]{4,3,2,1,0:T(8,128)(2,1)} %pa_ref.1, bf16[1,2,32,8,512]{4,3,2,1,0:T(8,128)(2,1)} %sw_ref.1, bf16[512,256]{1,0:T(8,128)(2,1)} %constant.28.za_ref, ...), custom_call_target="tpu_custom_call" | custom-call | tf_op jit(solution)/shard_map/analysis/pallas_call | solution.py:151
  14.4 0.0 copy-start.2
  14.4 28.2 %all_to_all.10.got_ref = bf16[128,24,128]{2,1,0:T(8,128)(2,1)} all-to-all(bf16[128,24,128]{2,1,0:T(8,128)(2,1)} %get-tuple-element.4), channel_id=1, replica_groups=mesh['dp'=4,'slab'=32] {'dp','slab'}, dimensions={0} | all-to-all | bytes 1572864 | tf_op jit(solution)/shard_map/all_to_all | solution.py:324
  42.5 3.9 %mix.1 = bf16[128,16,128]{2,1,0:T(8,128)(2,1)} custom-call(bf16[128,24,128]{2,1,0:T(8,128)(2,1)} %all_to_all.10.got_ref, bf16[4,256,256]{2,1,0:T(8,128)(2,1)} %constant.30.wf_ref, bf16[4,256,256]{2,1,0:T(8,128)(2,1)} %constant.31.wi_ref), custom_call_target="tpu_custom_call" | custom-call | tf_op jit(solution)/shard_map/mix/pallas_call | solution.py:226
  46.5 4.4 %all-to-all-start.1 = ((bf16[128,16,128]{2,1,0:T(8,128)(2,1)}), bf16[128,16,128]{2,1,0:T(8,128)(2,1)S(1)}, u32[]{:S(2)}, u32[]{:S(2)}) async-start(bf16[128,16,128]{2,1,0:T(8,128)(2,1)} %mix.1), calls=%async_computation.1 | async-start | bytes 1048576 | tf_op jit(solution)/shard_map/all_to_all | solution.py:328
  50.9 0.0 copy-done.2
  50.9 2.7 %collective-permute-start.2 = (bf16[2,32,512]{2,1,0:T(8,128)(2,1)S(1)}, bf16[2,32,512]{2,1,0:T(8,128)(2,1)S(1)}, u32[]{:S(2)}, u32[]{:S(2)}) collective-permute-start(bf16[2,32,512]{2,1,0:T(8,128)(2,1)S(1)} %bitcast.12), channel_id=1, source_target_pairs={{0,96},{32,64},{64,32},{96,0},{1,97},{33,65},{65,33},{97,1},{2,98}... | collective-permute-start | bytes 196616 | tf_op jit(solution)/shard_map/ppermute | solution.py:326
  53.7 0.5 collective-permute-start.1
  54.2 0.2 collective-permute-start
  54.3 0.0 copy-done
  54.3 6.9 %fusion.1 = bf16[4,128,128,32]{2,3,1,0:T(8,128)(2,1)} fusion(bf16[32,4,128,128]{3,2,1,0:T(8,128)(2,1)} %get-tuple-element.5, bf16[32,32]{1,0:T(8,128)(2,1)S(1)} %copy-done), kind=kOutput, calls=%fused_computation.2 | convolution fusion | flops 134217728 | bytes 8390656 | tf_op jit(solution)/shard_map/io,opyz->ipyz/dot_general | solution.py:327
  61.3 5.8 %copy.21 = bf16[4,128,128,32]{2,1,0,3:T(8,128)(2,1)} copy(bf16[4,128,128,32]{2,3,1,0:T(8,128)(2,1)} %fusion.1) | data formatting | bytes 8388608 | tf_op jit(solution)/shard_map/io,opyz->ipyz/dot_general | solution.py:327
  67.0 0.0 collective-permute-done.2.fm3
  67.0 0.0 copy-start.3
  67.0 0.0 collective-permute-done.1.fm2
  67.0 0.0 copy-start.4
  67.0 0.0 collective-permute-done.fm1
  67.1 0.0 copy-start.5
  67.1 0.0 all-to-all-done.1.got_ref
  67.1 0.0 copy-start.1
  67.1 0.6 copy-done.3
  67.6 0.0 copy-done.4
  67.7 0.0 copy-done.5
  67.7 0.2 copy-done.1
  67.9 9.8 %synthesis.1 = (bf16[1,32,4,128,128]{4,3,2,1,0:T(8,128)(2,1)}, f32[1,2,32,8,512]{4,3,2,1,0:T(8,128)}) custom-call(s32[1]{0:T(128)} %bitcast.me_ref, bf16[128,16,128]{2,1,0:T(8,128)(2,1)} %copy-done.1, bf16[32,4,128,128]{3,2,1,0:T(8,128)(2,1)} %bitcast.10, bf16[2,32,512]{2,1,0:T(8,128)(2,1)} %bitcast.11, bf16[2,32,512]{2,1,0:T(8,128)(2,1)} %copy-done.5, ...), custom_call_target="tpu_custom_call" | custom-call | tf_op jit(solution)/shard_map/synthesis/pallas_call | solution.py:291
Async XLA Ops:
  0.6 53.7 %copy-start = (bf16[32,32]{1,0:T(8,128)(2,1)S(1)}, bf16[32,32]{1,0:T(8,128)(2,1)}, u32[]{:S(2)}) copy-start(bf16[32,32]{1,0:T(8,128)(2,1)} %param.15) | copy-start | bytes 6148
  14.4 36.5 %copy-start.2 = (bf16[1,1,2,32,512]{4,3,2,1,0:T(8,128)(2,1)S(1)}, bf16[1,1,2,32,512]{4,3,2,1,0:T(8,128)(2,1)}, u32[]{:S(2)}) copy-start(bf16[1,1,2,32,512]{4,3,2,1,0:T(8,128)(2,1)} %param.13) | copy-start | bytes 196612
  46.5 20.6 %all-to-all-start.1 = ((bf16[128,16,128]{2,1,0:T(8,128)(2,1)}), bf16[128,16,128]{2,1,0:T(8,128)(2,1)S(1)}, u32[]{:S(2)}, u32[]{:S(2)}) async-start(bf16[128,16,128]{2,1,0:T(8,128)(2,1)} %mix.1), calls=%async_computation.1 | async-start | bytes 1048576 | tf_op jit(solution)/shard_map/all_to_all | solution.py:328
  50.9 16.1 %collective-permute-start.2 = (bf16[2,32,512]{2,1,0:T(8,128)(2,1)S(1)}, bf16[2,32,512]{2,1,0:T(8,128)(2,1)S(1)}, u32[]{:S(2)}, u32[]{:S(2)}) collective-permute-start(bf16[2,32,512]{2,1,0:T(8,128)(2,1)S(1)} %bitcast.12), channel_id=1, source_target_pairs={{0,96},{32,64},{64,32},{96,0},{1,97},{33,65},{65,33},{97,1},{2,98}... | collective-permute-start | bytes 196616 | tf_op jit(solution)/shard_map/ppermute | solution.py:326
  53.7 13.4 %collective-permute-start.1 = (bf16[2,32,512]{2,1,0:T(8,128)(2,1)S(1)}, bf16[2,32,512]{2,1,0:T(8,128)(2,1)S(1)}, u32[]{:S(2)}, u32[]{:S(2)}) collective-permute-start(bf16[2,32,512]{2,1,0:T(8,128)(2,1)S(1)} %bitcast.13), channel_id=1, source_target_pairs={{0,64},{32,96},{64,0},{96,32},{1,65},{33,97},{65,1},{97,33},{2,66}... | collective-permute-start | bytes 196616 | tf_op jit(solution)/shard_map/ppermute | solution.py:326
  54.2 12.9 %collective-permute-start = (bf16[2,32,512]{2,1,0:T(8,128)(2,1)S(1)}, bf16[2,32,512]{2,1,0:T(8,128)(2,1)S(1)}, u32[]{:S(2)}, u32[]{:S(2)}) collective-permute-start(bf16[2,32,512]{2,1,0:T(8,128)(2,1)S(1)} %bitcast.14), channel_id=1, source_target_pairs={{0,32},{32,0},{64,96},{96,64},{1,33},{33,1},{65,97},{97,65},{2,34}... | collective-permute-start | bytes 196616 | tf_op jit(solution)/shard_map/ppermute | solution.py:326
  67.0 0.6 copy-start.3
  67.0 0.6 copy-start.4
  67.1 0.7 copy-start.5
  67.1 0.8 %copy-start.1 = (bf16[128,16,128]{2,1,0:T(8,128)(2,1)}, bf16[128,16,128]{2,1,0:T(8,128)(2,1)S(1)}, u32[]{:S(2)}) copy-start(bf16[128,16,128]{2,1,0:T(8,128)(2,1)S(1)} %all-to-all-done.1.got_ref) | copy-start | bytes 1572868

commit v2 on v1

v2 whole, which is shorter than its diff:
```python
import functools
import math

import jax
import jax.numpy as jnp
import numpy as np
from jax import lax
from jax.experimental import pallas as pl
from jax.experimental.pallas import tpu as pltpu
from jax.sharding import PartitionSpec as P

C = 32
NP = 4
NY = 128
NZ = 128
KX = 32
KY = 32
KZ = 16
NB = 4
NS = 32
QL = 4
SHARE = C // NB
DEVS = NB * NS
STEPS = 8
CB = C // STEPS
AHEAD = 3
ALL = ("dp", "slab")
BF = jnp.bfloat16
F32 = jnp.float32
VMEM_LIMIT = 56 << 20


def kept(count, length):
    index = np.arange(count)
    return np.where(index < count // 2, index, length - count + index)


def angles(modes, length):
    return (modes[:, None] * np.arange(length)[None, :] % length) * (2.0 * math.pi / length)


def bf(table):
    return jnp.asarray(table, F32).astype(BF)


@functools.cache
def z_analysis():
    ang = angles(np.arange(KZ), NZ)
    weight = np.where(np.arange(KZ) == 0, 0.5, 1.0)[:, None] / math.sqrt(NY * NZ)
    real, imag = (np.cos(ang) * weight).T, (-np.sin(ang) * weight).T
    out = np.zeros((NP, NZ, 2, KZ, NP, 2), np.float32)
    for p in range(NP):
        out[p, :, 0, :, p, 0], out[p, :, 0, :, p, 1] = real, imag
        out[p, :, 1, :, p, 0], out[p, :, 1, :, p, 1] = imag, -real
    return out.reshape(NP * NZ, 2 * 128)


@functools.cache
def z_synthesis():
    ang = angles(np.arange(KZ), NZ)
    scale = 1.0 / math.sqrt(NY * NZ)
    cos, sin = np.cos(ang) * scale, np.sin(ang) * scale
    out = np.zeros((2, KZ, NP, 2, NP, NZ), np.float32)
    for p in range(NP):
        out[0, :, p, 0, p], out[0, :, p, 1, p] = cos, -sin
        out[1, :, p, 0, p], out[1, :, p, 1, p] = -sin, -cos
    return out.reshape(2 * 128, NP * NZ)


@functools.cache
def y_table():
    ang = angles(kept(KY, NY), NY)
    return np.concatenate([np.cos(ang), np.sin(ang)], 0).astype(np.float32)


@functools.cache
def x_table():
    nx = NS * NP
    ang = angles(kept(KX, nx), nx)
    cos, sin = np.cos(ang).T / math.sqrt(nx), np.sin(ang).T / math.sqrt(nx)
    out = np.zeros((nx, 2, 2, KX), np.float32)
    out[:, 0, 0], out[:, 0, 1], out[:, 1, 0], out[:, 1, 1] = cos, -sin, sin, cos
    return out


@functools.cache
def x_forward():
    out = np.zeros((QL, NS * NP, 2, 2, QL, KX), np.float32)
    for ql in range(QL):
        out[ql, :, :, :, ql] = x_table()
    return out.reshape(QL, 256, 256)


@functools.cache
def x_inverse():
    out = np.zeros((QL, 2, QL, KX, NS * NP, 2), np.float32)
    for ql in range(QL):
        out[ql, :, ql] = x_table().transpose(2, 3, 0, 1)
    return out.reshape(QL, 256, 256)


def dot(left, right):
    return jnp.dot(left, right, preferred_element_type=F32)


def twice_gelu_slope(x):
    bell = jnp.exp2(x * x * (-0.5 * math.log2(math.e)) + math.log2(2.0 * 0.3989422804014327))
    return 1.0 + (lax.erf(x * 0.7071067811865476) + x * bell)


def analysis_kernel(go_hbm, pa_hbm, sw_hbm, za_hbm, cs_ref, send_ref, za_ref, go_ref, pa_ref, sw_ref, even_ref, odd_ref, proj_ref, rows_ref, go_sem, pa_sem, sw_sem, za_sem):
    def fetch(n):
        part = pl.ds(n * CB, CB)
        return (
            pltpu.make_async_copy(go_hbm.at[0, part], go_ref.at[part], go_sem.at[n]),
            pltpu.make_async_copy(pa_hbm.at[0, part], pa_ref.at[part], pa_sem.at[n]),
        )

    def slope(step, left_ref):
        for c in range(CB):
            for p in range(NP):
                at = step * CB + c
                value = go_ref[at, p].astype(F32) * twice_gelu_slope(pa_ref[at, p].astype(F32))
                left_ref[p // 2, c * NY : (c + 1) * NY, (p % 2) * NZ : (p % 2 + 1) * NZ] = value.astype(BF)

    def transform(step, left_ref):
        tz = (dot(left_ref[0], za_ref[:256]) + dot(left_ref[1], za_ref[256:])).astype(BF)
        for c in range(CB):
            both = dot(cs_ref[...], tz[c * NY : (c + 1) * NY])
            proj_ref[pl.ds(((step + 1) * CB + c) * KY, KY), :] = both[:KY, :128] + both[KY:, 128:]

    def weights(step):
        j = step // 2
        lanes = pl.ds(pl.multiple_of((step % 2) * 256, 256), 256)
        block = sw_ref[step // 4, pl.ds((j % 2) * 16, 16), :, lanes].astype(F32).reshape(128, 256)
        for h in range(2):
            turned = block[:, h * 128 : (h + 1) * 128].T
            for qh in range(2):
                first = ((step % 2) * 4 + h * 2 + qh) * KZ
                for ql in range(QL):
                    at = (qh * QL + ql) * KZ
                    rows_ref[pl.ds(first * 24 + 8 + j * 4 + ql, KZ, stride=24), :] = turned[at : at + KZ]

    za_copy = pltpu.make_async_copy(za_hbm, za_ref, za_sem)
    sw_copy = pltpu.make_async_copy(sw_hbm.at[0], sw_ref, sw_sem)
    for n in range(AHEAD):
        for copy in fetch(n):
            copy.start()
        if n == 0:
            za_copy.start()
            sw_copy.start()
    odd_ref[...] = jnp.zeros_like(odd_ref)

    @pl.loop(0, STEPS // 2)
    def _(pair):
        for half, (now, before) in enumerate(((even_ref, odd_ref), (odd_ref, even_ref))):
            step = pair * 2 + half

            @pl.when(step + AHEAD < STEPS)
            def _():
                for copy in fetch(step + AHEAD):
                    copy.start()

            for copy in fetch(step):
                copy.wait()
            if half == 0:

                @pl.when(pair == 0)
                def _():
                    za_copy.wait()
                    sw_copy.wait()

            slope(step, now)
            transform(step - 1, before)
            weights(step)

    transform(STEPS - 1, odd_ref)
    for qh in range(KY // QL):
        group = [proj_ref[pl.ds(CB * KY + qh * QL + ql, C, stride=KY), :] for ql in range(QL)]
        turned = jnp.concatenate(group, 0).T
        for kz in range(KZ):
            rows_ref[pl.ds((qh * KZ + kz) * 24, 8), :] = turned[kz * 8 : kz * 8 + 8]
    send_ref[...] = rows_ref[...].reshape(DEVS, 24, 128).astype(BF)


def analysis(grad_out, pre_act, spec_weight):
    hbm = pl.BlockSpec(memory_space=pl.ANY)
    vmem = pl.BlockSpec(memory_space=pltpu.VMEM)
    return pl.pallas_call(
        analysis_kernel,
        in_specs=[hbm, hbm, hbm, hbm, vmem],
        out_specs=vmem,
        out_shape=jax.ShapeDtypeStruct((DEVS, 24, 128), BF),
        scratch_shapes=[
            pltpu.VMEM((NP * NZ, 256), BF),
            pltpu.VMEM((C, NP, NY, NZ), BF),
            pltpu.VMEM((C, NP, NY, NZ), BF),
            pltpu.VMEM((2, C, SHARE, KY * KZ), BF),
            pltpu.VMEM((2, CB * NY, 2 * NZ), BF),
            pltpu.VMEM((2, CB * NY, 2 * NZ), BF),
            pltpu.VMEM(((C + CB) * KY, 128), F32),
            pltpu.VMEM((DEVS * 24, 128), F32),
            pltpu.SemaphoreType.DMA((STEPS,)),
            pltpu.SemaphoreType.DMA((STEPS,)),
            pltpu.SemaphoreType.DMA,
            pltpu.SemaphoreType.DMA,
        ],
        compiler_params=pltpu.CompilerParams(vmem_limit_bytes=VMEM_LIMIT),
        name="analysis",
    )(grad_out, pre_act, spec_weight, bf(z_analysis()), bf(y_table()))


YB = 16


def local_kernel(w_ref, go_ref, pa_ref, out_ref, wide_ref):
    @pl.when(pl.program_id(0) == 0)
    def _():
        row = lax.broadcasted_iota(jnp.int32, (C * 8, C), 0)
        pick = jnp.where(row // 8 == lax.broadcasted_iota(jnp.int32, (C * 8, C), 1), 1.0, 0.0).astype(BF)
        spread = dot(dot(pick, w_ref[...]).astype(BF), pick.T)
        row = lax.broadcasted_iota(jnp.int32, (C * 8, C * 8), 0)
        column = lax.broadcasted_iota(jnp.int32, (C * 8, C * 8), 1)
        wide_ref[...] = jnp.where(row % 8 == column % 8, 0.5 * spread, 0.0).astype(BF)

    for p in range(NP):
        block = go_ref[0, :, p].astype(F32) * twice_gelu_slope(pa_ref[0, :, p].astype(F32))
        right = jnp.concatenate([block[:, h * 8 : h * 8 + 8].reshape(C * 8, NZ) for h in range(2)], 1).astype(BF)
        full = dot(wide_ref[...], right)
        halves = [full[:, h * NZ : (h + 1) * NZ].reshape(C, 8, NZ) for h in range(2)]
        out_ref[:, p] = jnp.concatenate(halves, 1).astype(BF)


def local_map(w_local, grad_out, pre_act):
    spec = pl.BlockSpec((1, C, NP, YB, NZ), lambda n: (0, 0, 0, n, 0))
    return pl.pallas_call(
        local_kernel,
        grid=(NY // YB,),
        in_specs=[pl.BlockSpec((C, C), lambda n: (0, 0)), spec, spec],
        out_specs=pl.BlockSpec((C, NP, YB, NZ), lambda n: (0, 0, n, 0)),
        out_shape=jax.ShapeDtypeStruct((C, NP, NY, NZ), BF),
        scratch_shapes=[pltpu.VMEM((C * 8, C * 8), BF)],
        compiler_params=pltpu.CompilerParams(vmem_limit_bytes=VMEM_LIMIT),
        cost_estimate=pl.CostEstimate(flops=2 * C * C * 8 * NP * NY * NZ, bytes_accessed=12 << 20, transcendentals=0),
        name="local_map",
    )(w_local, grad_out, pre_act)


def mix_kernel(got_ref, wf_ref, wi_ref, send_ref, rows_ref, v_ref, out_ref, g_ref, back_ref):
    rows_ref[...] = got_ref[...].astype(F32).reshape(DEVS * 24, 128)
    for j in range(4):
        for og in range(NB):
            first = og * NS * 24 + 8 + j * 4
            group = [rows_ref[pl.ds(first + ql, KX, stride=24), :] for ql in range(QL)]
            at = (j * NB + og) * 128
            v_ref[at : at + 128, :] = jnp.concatenate(group, 0).T

    planes = []
    for b in range(NB):
        part = [rows_ref[pl.ds((b * NS + s) * 24, 8), :] for s in range(NS)]
        planes.append(jnp.concatenate(part, 0).T.astype(BF))
    grad = jnp.zeros((NB * C, 256), F32)
    for ql in range(QL):
        left = jnp.concatenate([planes[b][ql * C : (ql + 1) * C] for b in range(NB)], 0)
        grad = grad + dot(left, wf_ref[ql])
    g_ref[...] = grad

    turned = grad.T
    for r in range(2):
        for ql in range(QL):
            at = (r * QL + ql) * KX
            for og in range(NB):
                first = og * NS * 16 + 8 + r * QL + ql
                out_ref[pl.ds(first, KX, stride=16), :] = turned[at : at + KX]

    for ig in range(4):
        acc = [[jnp.zeros((8, 128), F32) for _ in range(2)] for _ in range(NB)]
        for o in range(C):
            at = (o // SHARE) * 128 + (ig % 2) * 64 + o % SHARE
            vr = v_ref[pl.ds((ig // 2) * 512 + at, 8, stride=SHARE), :]
            vi = v_ref[pl.ds((2 + ig // 2) * 512 + at, 8, stride=SHARE), :]
            for b in range(NB):
                gr = g_ref[pl.ds(b * C + o, 1), :128]
                gi = g_ref[pl.ds(b * C + o, 1), 128:]
                acc[b][0] = acc[b][0] + gr * vr + gi * vi
                acc[b][1] = acc[b][1] + gi * vr - gr * vi
        for b in range(NB):
            back_ref[b * C + ig * 8 : b * C + ig * 8 + 8, :] = jnp.concatenate(acc[b], 1)

    back = back_ref[...].astype(BF)
    outs = [dot(back, wi_ref[ql]) for ql in range(QL)]
    for b in range(NB):
        turned = jnp.concatenate([outs[ql][b * C : (b + 1) * C] for ql in range(QL)], 0).T
        for s in range(NS):
            out_ref[pl.ds((b * NS + s) * 16, 8), :] = turned[s * 8 : s * 8 + 8]
    send_ref[...] = out_ref[...].reshape(DEVS, 16, 128).astype(BF)


def mix(got):
    return pl.pallas_call(
        mix_kernel,
        out_shape=jax.ShapeDtypeStruct((DEVS, 16, 128), BF),
        scratch_shapes=[
            pltpu.VMEM((DEVS * 24, 128), F32),
            pltpu.VMEM((16 * 128, 128), F32),
            pltpu.VMEM((DEVS * 16, 128), F32),
            pltpu.VMEM((128, 256), F32),
            pltpu.VMEM((128, 256), F32),
        ],
        compiler_params=pltpu.CompilerParams(vmem_limit_bytes=16 << 20),
        name="mix",
    )(got, bf(x_forward()), bf(x_inverse()))


def synthesis_kernel(me_ref, got_ref, local_hbm, fm0, fm1, fm2, fm3, cs_ref, zs_ref, out_hbm, spec_hbm, rows_ref, x_ref, g_ref, u_ref, local_ref, out_ref, spec_ref, in_sem, out_sem, spec_sem):
    me = me_ref[0]

    def fetch(n):
        part = pl.ds(n * CB, CB)
        return pltpu.make_async_copy(local_hbm.at[part], local_ref.at[part], in_sem.at[n])

    def store(n):
        part = pl.ds(n * CB, CB)
        return pltpu.make_async_copy(out_ref.at[part], out_hbm.at[0, part], out_sem.at[n])

    def spec_store(n):
        part = pl.ds(n * CB, CB)
        return pltpu.make_async_copy(spec_ref.at[:, part], spec_hbm.at[0, :, part], spec_sem.at[n])

    for n in range(STEPS):
        fetch(n).start()
    rows_ref[...] = got_ref[...].astype(F32).reshape(DEVS * 16, 128)
    for qh in range(KY // QL):
        group = [rows_ref[pl.ds((qh * KZ + kz) * 16, 8), :] for kz in range(KZ)]
        turned = jnp.concatenate(group, 0).T
        for ql in range(QL):
            x_ref[pl.ds(qh * QL + ql, C, stride=KY), :] = turned[ql * C : (ql + 1) * C]
    for r in range(2):
        for tile in range(4):
            group = []
            for q in range(2 * QL):
                first = (tile * 2 + q // QL) * KZ * 16 + 8 + r * QL + q % QL
                group.append(rows_ref[pl.ds(first, KZ, stride=16), :])
            g_ref[r, :, tile * 128 : (tile + 1) * 128] = jnp.concatenate(group, 0).T
    for hop, fm in enumerate((fm0, fm1, fm2, fm3)):
        u_ref[hop] = fm[...].astype(F32)

    @pl.loop(0, STEPS)
    def _(step):
        fetch(step).wait()
        for pair in range(CB // 2):
            first = (step * CB + pair * 2) * KY
            xs = jnp.concatenate([x_ref[pl.ds(first, KY), :], x_ref[pl.ds(first + KY, KY), :]], 1)
            uv = dot(cs_ref[...], xs.astype(BF)).astype(BF)
            left = [
                jnp.concatenate([uv[:NY, k * 128 : k * 128 + 128], uv[NY:, k * 128 : k * 128 + 128]], 1)
                for k in range(2)
            ]
            full = dot(jnp.concatenate(left, 0), zs_ref[...])
            for k in range(2):
                c = step * CB + pair * 2 + k
                for p in range(NP):
                    total = full[k * NY : (k + 1) * NY, p * NZ : (p + 1) * NZ] + local_ref[c, p].astype(F32)
                    out_ref[c, p] = total.astype(BF)
        store(step).start()

        for k in range(CB):
            i = step * CB + k
            wr, wi = jnp.zeros((SHARE, KY * KZ), F32), jnp.zeros((SHARE, KY * KZ), F32)
            for hop in range(NB):
                at = pl.multiple_of((me ^ hop) * C + me * SHARE, SHARE)
                gr, gi = g_ref[0, pl.ds(at, SHARE), :], g_ref[1, pl.ds(at, SHARE), :]
                ur, ui = u_ref[hop, 0, pl.ds(i, 1), :], u_ref[hop, 1, pl.ds(i, 1), :]
                wr = wr + gr * ur + gi * ui
                wi = wi + gi * ur - gr * ui
            spec_ref[0, i] = wr
            spec_ref[1, i] = wi
        spec_store(step).start()

    for n in range(STEPS):
        store(n).wait()
        spec_store(n).wait()


def synthesis(me, got, local, fms):
    hbm = pl.BlockSpec(memory_space=pl.ANY)
    vmem = pl.BlockSpec(memory_space=pltpu.VMEM)
    table = y_table().reshape(2, KY, NY).transpose(0, 2, 1).reshape(2 * NY, KY)
    return pl.pallas_call(
        synthesis_kernel,
        in_specs=[pl.BlockSpec(memory_space=pltpu.SMEM), vmem, hbm, *[vmem] * NB, vmem, vmem],
        out_specs=[hbm, hbm],
        out_shape=[
            jax.ShapeDtypeStruct((1, C, NP, NY, NZ), BF),
            jax.ShapeDtypeStruct((1, 2, C, SHARE, KY * KZ), F32),
        ],
        scratch_shapes=[
            pltpu.VMEM((DEVS * 16, 128), F32),
            pltpu.VMEM((C * KY, 128), F32),
            pltpu.VMEM((2, 128, KY * KZ), F32),
            pltpu.VMEM((NB, 2, C, KY * KZ), F32),
            pltpu.VMEM((C, NP, NY, NZ), BF),
            pltpu.VMEM((C, NP, NY, NZ), BF),
            pltpu.VMEM((2, C, SHARE, KY * KZ), F32),
            pltpu.SemaphoreType.DMA((STEPS,)),
            pltpu.SemaphoreType.DMA((STEPS,)),
            pltpu.SemaphoreType.DMA((STEPS,)),
        ],
        compiler_params=pltpu.CompilerParams(vmem_limit_bytes=51 << 20),
        name="synthesis",
    )(me, got, local, *fms, bf(table), bf(z_synthesis()))


def shards(grad_out, pre_act, forward_modes, spec_weight, w_local):
    me = lax.axis_index("dp")
    send = analysis(grad_out, pre_act, spec_weight)
    send, grad_out, pre_act = lax.optimization_barrier((send, grad_out, pre_act))
    got = lax.all_to_all(send, ALL, 0, 0, tiled=True)
    local = local_map(w_local, grad_out, pre_act)
    got, local = lax.optimization_barrier((got, local))
    fm = forward_modes.reshape(2, C, KY * KZ)
    fms = [fm] + [lax.ppermute(fm, "dp", [(b, b ^ hop) for b in range(NB)]) for hop in range(1, NB)]
    got = lax.all_to_all(mix(got), ALL, 0, 0, tiled=True)
    return synthesis(me.reshape(1), got, local, fms)


def solution(mesh):
    return jax.shard_map(
        shards,
        mesh=mesh,
        in_specs=(
            P("dp", None, "slab", None, None),
            P("dp", None, "slab", None, None),
            P("dp", "slab", None, None, None),
            P("slab", None, None, "dp", None),
            P(),
        ),
        out_specs=(P("dp", None, "slab", None, None), P("slab", None, None, "dp", None)),
        check_vma=False,
    )
```

time: 78.9 us -> 67.8 us (0.86)
  blocking collectives: 28.2 us -> 0 us
  waiting for transfers between devices: 0.01 us -> 16.5 us
  starting transfers between devices: 7.83 us -> 19.3 us
  matrix products: 6.93 us -> 0 us
  local copies, waits for them, and re-layouts: 6.6 us -> 0.03 us
  Pallas kernels: 27.5 us -> 30.8 us
    all_to_all x1 -> x0, blocking collectives: 28.2 us -> none  [shards(): got = lax.all_to_all(send, ALL, 0, 0, tiled=True)]
    all_to_all x0 -> x1, starting transfers between devices: none -> 11.5 us  [shards(): got = lax.all_to_all(send, ALL, 0, 0, tiled=True)]
    ppermute x3, waiting for transfers between devices: 0.01 us -> 7.99 us  [shards(): lax.ppermute(fm, 'dp', [(b, b ^ hop) for b in range(NB)])]
    dot_general x1 -> x0, matrix products: 6.93 us -> none  [shards(): jnp.einsum('io,opyz->ipyz', w_local, dpre, preferred_element_type=F32)]
    all_to_all x0 -> x1, waiting for transfers between devices: none -> 6.18 us  [shards(): got = lax.all_to_all(send, ALL, 0, 0, tiled=True)]
    dot_general x1 -> x0, local copies, waits for them, and re-layouts: 5.76 us -> none  [shards(): jnp.einsum('io,opyz->ipyz', w_local, dpre, preferred_element_type=F32)]
    pallas_call x2 -> x3, Pallas kernels: 23.5 us -> 28.2 us  [the longest x1 10.9 us: analysis(): pl.pallas_call(analysis_kernel, in_specs=[hbm, hbm, hbm, hbm, vmem], out_...]
    all_to_all x1, waiting for transfers between devices: 0.01 us -> 2.32 us  [shards(): got = lax.all_to_all(mix(got), ALL, 0, 0, tiled=True)]
  transfers between devices with their start and end apart: 4 -> 5, of which waited for: 0 -> 3; matrix products, arithmetic and copies ran while one was open for 16% -> 0% of each run, Pallas kernels for 0% -> 15%
where the time goes in v2:
time: 67.8 us; the launch traced here: 67.3 us
  Pallas kernels  30.8 us (45%)
  starting transfers between devices  19.3 us (28%)
  waiting for transfers between devices  16.5 us (24%)
  between operations  0.71 us (1%)
    all_to_all x1, starting transfers between devices, shards(): got = lax.all_to_all(send, ALL, 0, 0, tiled=True)  11.5 us
    pallas_call x1, Pallas kernels, analysis(): pl.pallas_call(analysis_kernel, in_specs=[hbm, hbm, hbm, hbm, vmem], out_...  10.9 us
    pallas_call x1, Pallas kernels, local_map(): pl.pallas_call(local_kernel, grid=(NY // YB,), in_specs=[pl.BlockSpec((C,...  10.3 us
    ppermute x3, waiting for transfers between devices, shards(): lax.ppermute(fm, 'dp', [(b, b ^ hop) for b in range(NB)])  7.99 us
    pallas_call x1, Pallas kernels, synthesis(): pl.pallas_call(synthesis_kernel, in_specs=[pl.BlockSpec(memory_space=pltp...  7.07 us
    all_to_all x1, waiting for transfers between devices, shards(): got = lax.all_to_all(send, ALL, 0, 0, tiled=True)  6.18 us
    all_to_all x1, starting transfers between devices, shards(): got = lax.all_to_all(mix(got), ALL, 0, 0, tiled=True)  4.42 us
    ppermute x3, starting transfers between devices, shards(): lax.ppermute(fm, 'dp', [(b, b ^ hop) for b in range(NB)])  3.41 us
  transfers between devices with their start and end apart: 5, of which 3 were waited for; matrix products, arithmetic and copies ran while one was open for 0% of the time, Pallas kernels for 15%

profile of v2, /device:TPU:1, one launch (start us, length us, event | category | flops | bytes accessed | tf_op | source)
XLA Modules:
  0.0 67.3 jit_solution(3734760745526045752)
XLA Ops:
  0.6 10.9 %analysis.1 = bf16[128,24,128]{2,1,0:T(8,128)(2,1)} custom-call(bf16[1,32,4,128,128]{4,3,2,1,0:T(8,128)(2,1)} %go_ref, bf16[1,32,4,128,128]{4,3,2,1,0:T(8,128)(2,1)} %pa_ref, bf16[1,2,32,8,512]{4,3,2,1,0:T(8,128)(2,1)} %sw_hbm.1, bf16[512,256]{1,0:T(8,128)(2,1)} %constant.28.za_hbm, bf16[64,128]{1,0:T(8,128)(2,1)} %constant.29.cs_ref), custom_call_target="tpu_custom_call" | custom-call | tf_op jit(solution)/shard_map/analysis/pallas_call | solution.py:189
  11.5 11.5 %all-to-all-start = ((bf16[128,24,128]{2,1,0:T(8,128)(2,1)}), bf16[128,24,128]{2,1,0:T(8,128)(2,1)S(1)}, u32[]{:S(2)}, u32[]{:S(2)}) async-start(bf16[128,24,128]{2,1,0:T(8,128)(2,1)} %analysis.1), calls=%async_computation | async-start | bytes 1572864 | tf_op jit(solution)/shard_map/all_to_all | solution.py:418
  23.0 0.0 copy-start
  23.0 0.0 copy-start.1
  23.0 0.0 copy-start.3
  23.0 0.0 copy-start.2
  23.1 0.0 copy-start.4
  23.1 10.3 %local_map.1.local_hbm = bf16[32,4,128,128]{3,2,1,0:T(8,128)(2,1)} custom-call(bf16[32,32]{1,0:T(8,128)(2,1)} %w_ref.1, bf16[1,32,4,128,128]{4,3,2,1,0:T(8,128)(2,1)} %go_ref, bf16[1,32,4,128,128]{4,3,2,1,0:T(8,128)(2,1)} %pa_ref), custom_call_target="tpu_custom_call" | custom-call | flops 1073741824 | bytes 12582912 | tf_op jit(solution)/shard_map/local_map/pallas_call | solution.py:236
  33.4 6.2 %all-to-all-done.got_ref = bf16[128,24,128]{2,1,0:T(8,128)(2,1)S(1)} async-done(((bf16[128,24,128]{2,1,0:T(8,128)(2,1)}), bf16[128,24,128]{2,1,0:T(8,128)(2,1)S(1)}, u32[]{:S(2)}, u32[]{:S(2)}) %all-to-all-start) | async-done | bytes 786464 | tf_op jit(solution)/shard_map/all_to_all | solution.py:418
  39.5 0.0 copy-done
  39.5 0.0 copy-done.1
  39.5 2.5 %mix.1 = bf16[128,16,128]{2,1,0:T(8,128)(2,1)} custom-call(bf16[128,24,128]{2,1,0:T(8,128)(2,1)S(1)} %all-to-all-done.got_ref, bf16[4,256,256]{2,1,0:T(8,128)(2,1)S(1)} %copy-done.1, bf16[4,256,256]{2,1,0:T(8,128)(2,1)S(1)} %copy-done), custom_call_target="tpu_custom_call" | custom-call | tf_op jit(solution)/shard_map/mix/pallas_call | solution.py:300
  42.1 4.4 %all-to-all-start.1 = ((bf16[128,16,128]{2,1,0:T(8,128)(2,1)}), bf16[128,16,128]{2,1,0:T(8,128)(2,1)S(1)}, u32[]{:S(2)}, u32[]{:S(2)}) async-start(bf16[128,16,128]{2,1,0:T(8,128)(2,1)} %mix.1), calls=%async_computation.1 | async-start | bytes 1048576 | tf_op jit(solution)/shard_map/all_to_all | solution.py:423
  46.5 0.0 copy-done.3
  46.5 2.7 %collective-permute-start.2 = (bf16[2,32,512]{2,1,0:T(8,128)(2,1)S(1)}, bf16[2,32,512]{2,1,0:T(8,128)(2,1)S(1)}, u32[]{:S(2)}, u32[]{:S(2)}) collective-permute-start(bf16[2,32,512]{2,1,0:T(8,128)(2,1)S(1)} %bitcast.2), channel_id=1, source_target_pairs={{0,96},{32,64},{64,32},{96,0},{1,97},{33,65},{65,33},{97,1},{2,98}... | collective-permute-start | bytes 196616 | tf_op jit(solution)/shard_map/ppermute | solution.py:422
  49.3 0.5 collective-permute-start.1
  49.8 0.2 collective-permute-start
  49.9 8.0 %collective-permute-done.2.fm3 = bf16[2,32,512]{2,1,0:T(8,128)(2,1)S(1)} collective-permute-done((bf16[2,32,512]{2,1,0:T(8,128)(2,1)S(1)}, bf16[2,32,512]{2,1,0:T(8,128)(2,1)S(1)}, u32[]{:S(2)}, u32[]{:S(2)}) %collective-permute-start.2) | collective-permute-done | bytes 65568 | tf_op jit(solution)/shard_map/ppermute | solution.py:422
  57.9 0.0 collective-permute-done.1.fm2
  57.9 0.0 collective-permute-done.fm1
  57.9 2.3 %all-to-all-done.1.got_ref = bf16[128,16,128]{2,1,0:T(8,128)(2,1)S(1)} async-done(((bf16[128,16,128]{2,1,0:T(8,128)(2,1)}), bf16[128,16,128]{2,1,0:T(8,128)(2,1)S(1)}, u32[]{:S(2)}, u32[]{:S(2)}) %all-to-all-start.1) | async-done | bytes 524320 | tf_op jit(solution)/shard_map/all_to_all | solution.py:423
  60.2 0.0 copy-done.2
  60.2 0.0 copy-done.4
  60.3 7.1 %synthesis.1 = (bf16[1,32,4,128,128]{4,3,2,1,0:T(8,128)(2,1)}, f32[1,2,32,8,512]{4,3,2,1,0:T(8,128)}) custom-call(s32[1]{0:T(128)} %bitcast.me_ref, bf16[128,16,128]{2,1,0:T(8,128)(2,1)S(1)} %all-to-all-done.1.got_ref, bf16[32,4,128,128]{3,2,1,0:T(8,128)(2,1)} %local_map.1.local_hbm, bf16[2,32,512]{2,1,0:T(8,128)(2,1)S(1)} %bitcast.5, ...), custom_call_target="tpu_custom_call" | custom-call | tf_op jit(solution)/shard_map/synthesis/pallas_call | solution.py:389
Async XLA Ops:
  11.5 28.0 %all-to-all-start = ((bf16[128,24,128]{2,1,0:T(8,128)(2,1)}), bf16[128,24,128]{2,1,0:T(8,128)(2,1)S(1)}, u32[]{:S(2)}, u32[]{:S(2)}) async-start(bf16[128,24,128]{2,1,0:T(8,128)(2,1)} %analysis.1), calls=%async_computation | async-start | bytes 1572864 | tf_op jit(solution)/shard_map/all_to_all | solution.py:418
  23.0 16.5 %copy-start = (bf16[4,256,256]{2,1,0:T(8,128)(2,1)S(1)}, bf16[4,256,256]{2,1,0:T(8,128)(2,1)}, u32[]{:S(2)}) copy-start(bf16[4,256,256]{2,1,0:T(8,128)(2,1)} %constant.31.wi_ref) | copy-start | bytes 1572868
  23.0 16.5 %copy-start.1 = (bf16[4,256,256]{2,1,0:T(8,128)(2,1)S(1)}, bf16[4,256,256]{2,1,0:T(8,128)(2,1)}, u32[]{:S(2)}) copy-start(bf16[4,256,256]{2,1,0:T(8,128)(2,1)} %constant.30.wf_ref) | copy-start | bytes 1572868
  23.0 23.5 %copy-start.3 = (bf16[1,1,2,32,512]{4,3,2,1,0:T(8,128)(2,1)S(1)}, bf16[1,1,2,32,512]{4,3,2,1,0:T(8,128)(2,1)}, u32[]{:S(2)}) copy-start(bf16[1,1,2,32,512]{4,3,2,1,0:T(8,128)(2,1)} %param.13) | copy-start | bytes 196612
  23.0 37.2 %copy-start.2 = (bf16[256,512]{1,0:T(8,128)(2,1)S(1)}, bf16[256,512]{1,0:T(8,128)(2,1)}, u32[]{:S(2)}) copy-start(bf16[256,512]{1,0:T(8,128)(2,1)} %constant.33.zs_ref) | copy-start | bytes 786436
  23.1 37.2 %copy-start.4 = (bf16[256,32]{1,0:T(8,128)(2,1)S(1)}, bf16[256,32]{1,0:T(8,128)(2,1)}, u32[]{:S(2)}) copy-start(bf16[256,32]{1,0:T(8,128)(2,1)} %constant.32.cs_ref) | copy-start | bytes 49156
  42.1 18.2 %all-to-all-start.1 = ((bf16[128,16,128]{2,1,0:T(8,128)(2,1)}), bf16[128,16,128]{2,1,0:T(8,128)(2,1)S(1)}, u32[]{:S(2)}, u32[]{:S(2)}) async-start(bf16[128,16,128]{2,1,0:T(8,128)(2,1)} %mix.1), calls=%async_computation.1 | async-start | bytes 1048576 | tf_op jit(solution)/shard_map/all_to_all | solution.py:423
  46.5 11.4 %collective-permute-start.2 = (bf16[2,32,512]{2,1,0:T(8,128)(2,1)S(1)}, bf16[2,32,512]{2,1,0:T(8,128)(2,1)S(1)}, u32[]{:S(2)}, u32[]{:S(2)}) collective-permute-start(bf16[2,32,512]{2,1,0:T(8,128)(2,1)S(1)} %bitcast.2), channel_id=1, source_target_pairs={{0,96},{32,64},{64,32},{96,0},{1,97},{33,65},{65,33},{97,1},{2,98}... | collective-permute-start | bytes 196616 | tf_op jit(solution)/shard_map/ppermute | solution.py:422
  49.3 8.7 %collective-permute-start.1 = (bf16[2,32,512]{2,1,0:T(8,128)(2,1)S(1)}, bf16[2,32,512]{2,1,0:T(8,128)(2,1)S(1)}, u32[]{:S(2)}, u32[]{:S(2)}) collective-permute-start(bf16[2,32,512]{2,1,0:T(8,128)(2,1)S(1)} %bitcast.3), channel_id=1, source_target_pairs={{0,64},{32,96},{64,0},{96,32},{1,65},{33,97},{65,1},{97,33},{2,66}... | collective-permute-start | bytes 196616 | tf_op jit(solution)/shard_map/ppermute | solution.py:422
  49.8 8.1 %collective-permute-start = (bf16[2,32,512]{2,1,0:T(8,128)(2,1)S(1)}, bf16[2,32,512]{2,1,0:T(8,128)(2,1)S(1)}, u32[]{:S(2)}, u32[]{:S(2)}) collective-permute-start(bf16[2,32,512]{2,1,0:T(8,128)(2,1)S(1)} %bitcast.4), channel_id=1, source_target_pairs={{0,32},{32,0},{64,96},{96,64},{1,33},{33,1},{65,97},{97,65},{2,34}... | collective-permute-start | bytes 196616 | tf_op jit(solution)/shard_map/ppermute | solution.py:422

commit v3 on v2

--- a/solution.py
+++ b/solution.py
@@ -23,7 +23,9 @@
 DEVS = NB * NS
 STEPS = 8
 CB = C // STEPS
-AHEAD = 3
+AHEAD = 2
+SIZES = (8, 8, 8, 8)
+STARTS = tuple(sum(SIZES[:n]) for n in range(len(SIZES)))
 ALL = ("dp", "slab")
 BF = jnp.bfloat16
 F32 = jnp.float32
@@ -108,38 +110,40 @@
     return 1.0 + (lax.erf(x * 0.7071067811865476) + x * bell)
 
 
-def analysis_kernel(go_hbm, pa_hbm, sw_hbm, za_hbm, cs_ref, send_ref, za_ref, go_ref, pa_ref, sw_ref, even_ref, odd_ref, proj_ref, rows_ref, go_sem, pa_sem, sw_sem, za_sem):
+def analysis_kernel(go_hbm, pa_hbm, sw_hbm, za_hbm, cs_ref, send_hbm, za_ref, go_ref, pa_ref, sw_ref, even_ref, odd_ref, proj_ref, rows_ref, send_ref, go_sem, pa_sem, sw_sem, za_sem, out_sem):
     def fetch(n):
-        part = pl.ds(n * CB, CB)
+        part = pl.ds(STARTS[n], SIZES[n])
         return (
             pltpu.make_async_copy(go_hbm.at[0, part], go_ref.at[part], go_sem.at[n]),
             pltpu.make_async_copy(pa_hbm.at[0, part], pa_ref.at[part], pa_sem.at[n]),
         )
 
-    def slope(step, left_ref):
-        for c in range(CB):
+    def slope(n, left_ref):
+        for copy in fetch(n):
+            copy.wait()
+        for c in range(SIZES[n]):
             for p in range(NP):
-                at = step * CB + c
+                at = STARTS[n] + c
                 value = go_ref[at, p].astype(F32) * twice_gelu_slope(pa_ref[at, p].astype(F32))
                 left_ref[p // 2, c * NY : (c + 1) * NY, (p % 2) * NZ : (p % 2 + 1) * NZ] = value.astype(BF)
 
-    def transform(step, left_ref):
-        tz = (dot(left_ref[0], za_ref[:256]) + dot(left_ref[1], za_ref[256:])).astype(BF)
-        for c in range(CB):
+    def transform(n, left_ref):
+        rows = SIZES[n] * NY
+        tz = (dot(left_ref[0, :rows], za_ref[:256]) + dot(left_ref[1, :rows], za_ref[256:])).astype(BF)
+        for c in range(SIZES[n]):
             both = dot(cs_ref[...], tz[c * NY : (c + 1) * NY])
-            proj_ref[pl.ds(((step + 1) * CB + c) * KY, KY), :] = both[:KY, :128] + both[KY:, 128:]
-
-    def weights(step):
-        j = step // 2
-        lanes = pl.ds(pl.multiple_of((step % 2) * 256, 256), 256)
-        block = sw_ref[step // 4, pl.ds((j % 2) * 16, 16), :, lanes].astype(F32).reshape(128, 256)
-        for h in range(2):
-            turned = block[:, h * 128 : (h + 1) * 128].T
-            for qh in range(2):
-                first = ((step % 2) * 4 + h * 2 + qh) * KZ
-                for ql in range(QL):
-                    at = (qh * QL + ql) * KZ
-                    rows_ref[pl.ds(first * 24 + 8 + j * 4 + ql, KZ, stride=24), :] = turned[at : at + KZ]
+            at = (STARTS[n] + c) * KY
+            proj_ref[at : at + KY, :] = both[:KY, :128] + both[KY:, 128:]
+
+    def weights(n):
+        j, tile = n // 4, n % 4
+        block = sw_ref[j // 2, (j % 2) * 16 : (j % 2) * 16 + 16, :, tile * 128 : tile * 128 + 128]
+        turned = block.astype(F32).reshape(128, 128).T
+        for qh in range(2):
+            first = (tile * 2 + qh) * KZ
+            for ql in range(QL):
+                at = (qh * QL + ql) * KZ
+                rows_ref[pl.ds(first * 24 + 8 + j * 4 + ql, KZ, stride=24), :] = turned[at : at + KZ]
 
     za_copy = pltpu.make_async_copy(za_hbm, za_ref, za_sem)
     sw_copy = pltpu.make_async_copy(sw_hbm.at[0], sw_ref, sw_sem)
@@ -149,38 +153,34 @@
         if n == 0:
             za_copy.start()
             sw_copy.start()
-    odd_ref[...] = jnp.zeros_like(odd_ref)
-
-    @pl.loop(0, STEPS // 2)
-    def _(pair):
-        for half, (now, before) in enumerate(((even_ref, odd_ref), (odd_ref, even_ref))):
-            step = pair * 2 + half
-
-            @pl.when(step + AHEAD < STEPS)
-            def _():
-                for copy in fetch(step + AHEAD):
-                    copy.start()
-
-            for copy in fetch(step):
-                copy.wait()
-            if half == 0:
-
-                @pl.when(pair == 0)
-                def _():
-                    za_copy.wait()
-                    sw_copy.wait()
-
-            slope(step, now)
-            transform(step - 1, before)
-            weights(step)
-
-    transform(STEPS - 1, odd_ref)
+    buffers = (even_ref, odd_ref)
+    for n in range(len(SIZES)):
+        if n + AHEAD < len(SIZES):
+            for copy in fetch(n + AHEAD):
+                copy.start()
+        if n == 1:
+            za_copy.wait()
+            sw_copy.wait()
+        slope(n, buffers[n % 2])
+        if n > 0:
+            transform(n - 1, buffers[(n - 1) % 2])
+            for tile in range(16):
+                if tile * (len(SIZES) - 1) // 16 == n - 1:
+                    weights(tile)
+    transform(len(SIZES) - 1, buffers[(len(SIZES) - 1) % 2])
+
+    outs = []
     for qh in range(KY // QL):
-        group = [proj_ref[pl.ds(CB * KY + qh * QL + ql, C, stride=KY), :] for ql in range(QL)]
+        group = [proj_ref[pl.ds(qh * QL + ql, C, stride=KY), :] for ql in range(QL)]
         turned = jnp.concatenate(group, 0).T
         for kz in range(KZ):
             rows_ref[pl.ds((qh * KZ + kz) * 24, 8), :] = turned[kz * 8 : kz * 8 + 8]
-    send_ref[...] = rows_ref[...].reshape(DEVS, 24, 128).astype(BF)
+        part = pl.ds(qh * KZ, KZ)
+        send_ref[part] = rows_ref[pl.ds(qh * KZ * 24, KZ * 24), :].reshape(KZ, 24, 128).astype(BF)
+        outs.append(pltpu.make_async_copy(send_ref.at[part], send_hbm.at[part], out_sem.at[qh]))
+        outs[-1].start()
+    for copy in outs:
+        copy.wait()
 
 
 def analysis(grad_out, pre_act, spec_weight):
@@ -189,28 +189,30 @@
     return pl.pallas_call(
         analysis_kernel,
         in_specs=[hbm, hbm, hbm, hbm, vmem],
-        out_specs=vmem,
+        out_specs=hbm,
         out_shape=jax.ShapeDtypeStruct((DEVS, 24, 128), BF),
         scratch_shapes=[
             pltpu.VMEM((NP * NZ, 256), BF),
             pltpu.VMEM((C, NP, NY, NZ), BF),
             pltpu.VMEM((C, NP, NY, NZ), BF),
             pltpu.VMEM((2, C, SHARE, KY * KZ), BF),
-            pltpu.VMEM((2, CB * NY, 2 * NZ), BF),
-            pltpu.VMEM((2, CB * NY, 2 * NZ), BF),
-            pltpu.VMEM(((C + CB) * KY, 128), F32),
+            pltpu.VMEM((2, max(SIZES) * NY, 2 * NZ), BF),
+            pltpu.VMEM((2, max(SIZES) * NY, 2 * NZ), BF),
+            pltpu.VMEM((C * KY, 128), F32),
             pltpu.VMEM((DEVS * 24, 128), F32),
-            pltpu.SemaphoreType.DMA((STEPS,)),
-            pltpu.SemaphoreType.DMA((STEPS,)),
+            pltpu.VMEM((DEVS, 24, 128), BF),
+            pltpu.SemaphoreType.DMA((len(SIZES),)),
+            pltpu.SemaphoreType.DMA((len(SIZES),)),
             pltpu.SemaphoreType.DMA,
             pltpu.SemaphoreType.DMA,
+            pltpu.SemaphoreType.DMA((KY // QL,)),
         ],
         compiler_params=pltpu.CompilerParams(vmem_limit_bytes=VMEM_LIMIT),
         name="analysis",
     )(grad_out, pre_act, spec_weight, bf(z_analysis()), bf(y_table()))
 
 
-YB = 16
+YB = 32
 
 
 def local_kernel(w_ref, go_ref, pa_ref, out_ref, wide_ref):
@@ -225,9 +227,9 @@
 
     for p in range(NP):
         block = go_ref[0, :, p].astype(F32) * twice_gelu_slope(pa_ref[0, :, p].astype(F32))
-        right = jnp.concatenate([block[:, h * 8 : h * 8 + 8].reshape(C * 8, NZ) for h in range(2)], 1).astype(BF)
+        right = jnp.concatenate([block[:, h * 8 : h * 8 + 8].reshape(C * 8, NZ) for h in range(YB // 8)], 1).astype(BF)
         full = dot(wide_ref[...], right)
-        halves = [full[:, h * NZ : (h + 1) * NZ].reshape(C, 8, NZ) for h in range(2)]
+        halves = [full[:, h * NZ : (h + 1) * NZ].reshape(C, 8, NZ) for h in range(YB // 8)]
         out_ref[:, p] = jnp.concatenate(halves, 1).astype(BF)
 
 
@@ -312,7 +314,7 @@
     )(got, bf(x_forward()), bf(x_inverse()))
 
 
-def synthesis_kernel(me_ref, got_ref, local_hbm, fm0, fm1, fm2, fm3, cs_ref, zs_ref, out_hbm, spec_hbm, rows_ref, x_ref, g_ref, u_ref, local_ref, out_ref, spec_ref, in_sem, out_sem, spec_sem):
+def synthesis_kernel(me_ref, got_ref, local_hbm, fm0, fm1, fm2, fm3, cs_ref, zs_ref, out_hbm, spec_hbm, rows_ref, x_ref, g_ref, u_ref, uv_ref, local_ref, out_ref, spec_ref, in_sem, out_sem, spec_sem):
     me = me_ref[0]
 
     def fetch(n):
@@ -345,23 +347,26 @@
     for hop, fm in enumerate((fm0, fm1, fm2, fm3)):
         u_ref[hop] = fm[...].astype(F32)
 
+    for pair in range(C // 2):
+        first = pair * 2 * KY
+        xs = jnp.concatenate([x_ref[first : first + KY, :], x_ref[first + KY : first + 2 * KY, :]], 1)
+        uv = dot(cs_ref[...], xs.astype(BF)).astype(BF)
+        for k in range(2):
+            uv_ref[pair * 2 + k, :, :128] = uv[:NY, k * 128 : k * 128 + 128]
+            uv_ref[pair * 2 + k, :, 128:] = uv[NY:, k * 128 : k * 128 + 128]
+
     @pl.loop(0, STEPS)
     def _(step):
         fetch(step).wait()
-        for pair in range(CB // 2):
-            first = (step * CB + pair * 2) * KY
-            xs = jnp.concatenate([x_ref[pl.ds(first, KY), :], x_ref[pl.ds(first + KY, KY), :]], 1)
-            uv = dot(cs_ref[...], xs.astype(BF)).astype(BF)
-            left = [
-                jnp.concatenate([uv[:NY, k * 128 : k * 128 + 128], uv[NY:, k * 128 : k * 128 + 128]], 1)
-                for k in range(2)
-            ]
-            full = dot(jnp.concatenate(left, 0), zs_ref[...])
-            for k in range(2):
-                c = step * CB + pair * 2 + k
-                for p in range(NP):
-                    total = full[k * NY : (k + 1) * NY, p * NZ : (p + 1) * NZ] + local_ref[c, p].astype(F32)
-                    out_ref[c, p] = total.astype(BF)
+        left = uv_ref[pl.ds(step * CB, CB)].reshape(CB * NY, 256)
+        for p in range(NP):
+            if p % 2 == 0:
+                wide = dot(left, zs_ref[:, p * NZ : (p + 2) * NZ])
+            full = wide[:, (p % 2) * NZ : (p % 2 + 1) * NZ]
+            for k in range(CB):
+                c = step * CB + k
+                total = full[k * NY : (k + 1) * NY] + local_ref[c, p].astype(F32)
+                out_ref[c, p] = total.astype(BF)
         store(step).start()
 
         for k in range(CB):
@@ -399,6 +404,7 @@
             pltpu.VMEM((C * KY, 128), F32),
             pltpu.VMEM((2, 128, KY * KZ), F32),
             pltpu.VMEM((NB, 2, C, KY * KZ), F32),
+            pltpu.VMEM((C, NY, 256), BF),
             pltpu.VMEM((C, NP, NY, NZ), BF),
             pltpu.VMEM((C, NP, NY, NZ), BF),
             pltpu.VMEM((2, C, SHARE, KY * KZ), F32),

time: 67.8 us -> 63.5 us (0.937)
  Pallas kernels: 30.8 us -> 24.8 us
  waiting for transfers between devices: 16.5 us -> 18.2 us
    pallas_call x1, Pallas kernels: 7.07 us -> 4.74 us  [synthesis(): pl.pallas_call(synthesis_kernel, in_specs=[pl.BlockSpec(memory_space=pltp...]
    pallas_call x1, Pallas kernels: 10.9 us -> 8.99 us  [analysis(): pl.pallas_call(analysis_kernel, in_specs=[hbm, hbm, hbm, hbm, vmem], out_...]
    all_to_all x1, waiting for transfers between devices: 6.18 us -> 7.89 us  [shards(): got = lax.all_to_all(send, ALL, 0, 0, tiled=True)]
    pallas_call x1, Pallas kernels: 10.3 us -> 8.59 us  [local_map(): pl.pallas_call(local_kernel, grid=(NY // YB,), in_specs=[pl.BlockSpec((C,...]
  transfers between devices with their start and end apart: 5 -> 5, of which waited for: 3 -> 3; matrix products, arithmetic and copies ran while one was open for 0% -> 0% of each run, Pallas kernels for 15% -> 14%
where the time goes in v3:
time: 63.5 us; the launch traced here: 63.1 us
  Pallas kernels  24.8 us (39%)
  starting transfers between devices  19.3 us (30%)
  waiting for transfers between devices  18.2 us (29%)
  between operations  0.71 us (1%)
    all_to_all x1, starting transfers between devices, shards(): got = lax.all_to_all(send, ALL, 0, 0, tiled=True)  11.5 us
    pallas_call x1, Pallas kernels, analysis(): pl.pallas_call(analysis_kernel, in_specs=[hbm, hbm, hbm, hbm, vmem], out_...  8.99 us
    pallas_call x1, Pallas kernels, local_map(): pl.pallas_call(local_kernel, grid=(NY // YB,), in_specs=[pl.BlockSpec((C,...  8.59 us
    ppermute x3, waiting for transfers between devices, shards(): lax.ppermute(fm, 'dp', [(b, b ^ hop) for b in range(NB)])  7.99 us
    all_to_all x1, waiting for transfers between devices, shards(): got = lax.all_to_all(send, ALL, 0, 0, tiled=True)  7.89 us
    pallas_call x1, Pallas kernels, synthesis(): pl.pallas_call(synthesis_kernel, in_specs=[pl.BlockSpec(memory_space=pltp...  4.74 us
    all_to_all x1, starting transfers between devices, shards(): got = lax.all_to_all(mix(got), ALL, 0, 0, tiled=True)  4.42 us
    ppermute x3, starting transfers between devices, shards(): lax.ppermute(fm, 'dp', [(b, b ^ hop) for b in range(NB)])  3.41 us
  transfers between devices with their start and end apart: 5, of which 3 were waited for; matrix products, arithmetic and copies ran while one was open for 0% of the time, Pallas kernels for 14%

profile of v3, /device:TPU:1, one launch (start us, length us, event | category | flops | bytes accessed | tf_op | source)
XLA Modules:
  0.0 63.1 jit_solution(5903287461393687793)
XLA Ops:
  0.6 9.0 %analysis.1 = bf16[128,24,128]{2,1,0:T(8,128)(2,1)} custom-call(bf16[1,32,4,128,128]{4,3,2,1,0:T(8,128)(2,1)} %go_ref, bf16[1,32,4,128,128]{4,3,2,1,0:T(8,128)(2,1)} %pa_ref, bf16[1,2,32,8,512]{4,3,2,1,0:T(8,128)(2,1)} %sw_hbm.1, bf16[512,256]{1,0:T(8,128)(2,1)} %constant.28.za_hbm, bf16[64,128]{1,0:T(8,128)(2,1)} %constant.29.cs_ref), custom_call_target="tpu_custom_call" | custom-call | tf_op jit(solution)/shard_map/analysis/pallas_call | solution.py:189
  9.6 11.5 %all-to-all-start = ((bf16[128,24,128]{2,1,0:T(8,128)(2,1)}), bf16[128,24,128]{2,1,0:T(8,128)(2,1)S(1)}, u32[]{:S(2)}, u32[]{:S(2)}) async-start(bf16[128,24,128]{2,1,0:T(8,128)(2,1)} %analysis.1), calls=%async_computation | async-start | bytes 1572864 | tf_op jit(solution)/shard_map/all_to_all | solution.py:424
  21.1 0.0 copy-start
  21.1 0.0 copy-start.1
  21.2 0.0 copy-start.3
  21.2 0.0 copy-start.2
  21.2 0.0 copy-start.4
  21.2 8.6 %local_map.1.local_hbm = bf16[32,4,128,128]{3,2,1,0:T(8,128)(2,1)} custom-call(bf16[32,32]{1,0:T(8,128)(2,1)} %w_ref.1, bf16[1,32,4,128,128]{4,3,2,1,0:T(8,128)(2,1)} %go_ref, bf16[1,32,4,128,128]{4,3,2,1,0:T(8,128)(2,1)} %pa_ref), custom_call_target="tpu_custom_call" | custom-call | flops 1073741824 | bytes 12582912 | tf_op jit(solution)/shard_map/local_map/pallas_call | solution.py:238
  29.8 7.9 %all-to-all-done.got_ref = bf16[128,24,128]{2,1,0:T(8,128)(2,1)S(1)} async-done(((bf16[128,24,128]{2,1,0:T(8,128)(2,1)}), bf16[128,24,128]{2,1,0:T(8,128)(2,1)S(1)}, u32[]{:S(2)}, u32[]{:S(2)}) %all-to-all-start) | async-done | bytes 786464 | tf_op jit(solution)/shard_map/all_to_all | solution.py:424
  37.7 0.0 copy-done
  37.7 0.0 copy-done.1
  37.7 2.5 %mix.1 = bf16[128,16,128]{2,1,0:T(8,128)(2,1)} custom-call(bf16[128,24,128]{2,1,0:T(8,128)(2,1)S(1)} %all-to-all-done.got_ref, bf16[4,256,256]{2,1,0:T(8,128)(2,1)S(1)} %copy-done.1, bf16[4,256,256]{2,1,0:T(8,128)(2,1)S(1)} %copy-done), custom_call_target="tpu_custom_call" | custom-call | tf_op jit(solution)/shard_map/mix/pallas_call | solution.py:302
  40.2 4.4 %all-to-all-start.1 = ((bf16[128,16,128]{2,1,0:T(8,128)(2,1)}), bf16[128,16,128]{2,1,0:T(8,128)(2,1)S(1)}, u32[]{:S(2)}, u32[]{:S(2)}) async-start(bf16[128,16,128]{2,1,0:T(8,128)(2,1)} %mix.1), calls=%async_computation.1 | async-start | bytes 1048576 | tf_op jit(solution)/shard_map/all_to_all | solution.py:429
  44.6 0.0 copy-done.3
  44.6 2.7 %collective-permute-start.2 = (bf16[2,32,512]{2,1,0:T(8,128)(2,1)S(1)}, bf16[2,32,512]{2,1,0:T(8,128)(2,1)S(1)}, u32[]{:S(2)}, u32[]{:S(2)}) collective-permute-start(bf16[2,32,512]{2,1,0:T(8,128)(2,1)S(1)} %bitcast.2), channel_id=1, source_target_pairs={{0,96},{32,64},{64,32},{96,0},{1,97},{33,65},{65,33},{97,1},{2,98}... | collective-permute-start | bytes 196616 | tf_op jit(solution)/shard_map/ppermute | solution.py:428
  47.4 0.5 collective-permute-start.1
  47.9 0.2 collective-permute-start
  48.1 8.0 %collective-permute-done.2.fm3 = bf16[2,32,512]{2,1,0:T(8,128)(2,1)S(1)} collective-permute-done((bf16[2,32,512]{2,1,0:T(8,128)(2,1)S(1)}, bf16[2,32,512]{2,1,0:T(8,128)(2,1)S(1)}, u32[]{:S(2)}, u32[]{:S(2)}) %collective-permute-start.2) | collective-permute-done | bytes 65568 | tf_op jit(solution)/shard_map/ppermute | solution.py:428
  56.0 0.0 collective-permute-done.1.fm2
  56.0 0.0 collective-permute-done.fm1
  56.1 2.3 %all-to-all-done.1.got_ref = bf16[128,16,128]{2,1,0:T(8,128)(2,1)S(1)} async-done(((bf16[128,16,128]{2,1,0:T(8,128)(2,1)}), bf16[128,16,128]{2,1,0:T(8,128)(2,1)S(1)}, u32[]{:S(2)}, u32[]{:S(2)}) %all-to-all-start.1) | async-done | bytes 524320 | tf_op jit(solution)/shard_map/all_to_all | solution.py:429
  58.4 0.0 copy-done.2
  58.4 0.0 copy-done.4
  58.4 4.7 %synthesis.1 = (bf16[1,32,4,128,128]{4,3,2,1,0:T(8,128)(2,1)}, f32[1,2,32,8,512]{4,3,2,1,0:T(8,128)}) custom-call(s32[1]{0:T(128)} %bitcast.me_ref, bf16[128,16,128]{2,1,0:T(8,128)(2,1)S(1)} %all-to-all-done.1.got_ref, bf16[32,4,128,128]{3,2,1,0:T(8,128)(2,1)} %local_map.1.local_hbm, bf16[2,32,512]{2,1,0:T(8,128)(2,1)S(1)} %bitcast.5, ...), custom_call_target="tpu_custom_call" | custom-call | tf_op jit(solution)/shard_map/synthesis/pallas_call | solution.py:394
Async XLA Ops:
  9.6 28.0 %all-to-all-start = ((bf16[128,24,128]{2,1,0:T(8,128)(2,1)}), bf16[128,24,128]{2,1,0:T(8,128)(2,1)S(1)}, u32[]{:S(2)}, u32[]{:S(2)}) async-start(bf16[128,24,128]{2,1,0:T(8,128)(2,1)} %analysis.1), calls=%async_computation | async-start | bytes 1572864 | tf_op jit(solution)/shard_map/all_to_all | solution.py:424
  21.1 16.5 %copy-start = (bf16[4,256,256]{2,1,0:T(8,128)(2,1)S(1)}, bf16[4,256,256]{2,1,0:T(8,128)(2,1)}, u32[]{:S(2)}) copy-start(bf16[4,256,256]{2,1,0:T(8,128)(2,1)} %constant.31.wi_ref) | copy-start | bytes 1572868
  21.1 16.5 %copy-start.1 = (bf16[4,256,256]{2,1,0:T(8,128)(2,1)S(1)}, bf16[4,256,256]{2,1,0:T(8,128)(2,1)}, u32[]{:S(2)}) copy-start(bf16[4,256,256]{2,1,0:T(8,128)(2,1)} %constant.30.wf_ref) | copy-start | bytes 1572868
  21.2 23.5 %copy-start.3 = (bf16[1,1,2,32,512]{4,3,2,1,0:T(8,128)(2,1)S(1)}, bf16[1,1,2,32,512]{4,3,2,1,0:T(8,128)(2,1)}, u32[]{:S(2)}) copy-start(bf16[1,1,2,32,512]{4,3,2,1,0:T(8,128)(2,1)} %param.13) | copy-start | bytes 196612
  21.2 37.2 %copy-start.2 = (bf16[256,512]{1,0:T(8,128)(2,1)S(1)}, bf16[256,512]{1,0:T(8,128)(2,1)}, u32[]{:S(2)}) copy-start(bf16[256,512]{1,0:T(8,128)(2,1)} %constant.33.zs_ref) | copy-start | bytes 786436
  21.2 37.2 %copy-start.4 = (bf16[256,32]{1,0:T(8,128)(2,1)S(1)}, bf16[256,32]{1,0:T(8,128)(2,1)}, u32[]{:S(2)}) copy-start(bf16[256,32]{1,0:T(8,128)(2,1)} %constant.32.cs_ref) | copy-start | bytes 49156
  40.2 18.2 %all-to-all-start.1 = ((bf16[128,16,128]{2,1,0:T(8,128)(2,1)}), bf16[128,16,128]{2,1,0:T(8,128)(2,1)S(1)}, u32[]{:S(2)}, u32[]{:S(2)}) async-start(bf16[128,16,128]{2,1,0:T(8,128)(2,1)} %mix.1), calls=%async_computation.1 | async-start | bytes 1048576 | tf_op jit(solution)/shard_map/all_to_all | solution.py:429
  44.6 11.4 %collective-permute-start.2 = (bf16[2,32,512]{2,1,0:T(8,128)(2,1)S(1)}, bf16[2,32,512]{2,1,0:T(8,128)(2,1)S(1)}, u32[]{:S(2)}, u32[]{:S(2)}) collective-permute-start(bf16[2,32,512]{2,1,0:T(8,128)(2,1)S(1)} %bitcast.2), channel_id=1, source_target_pairs={{0,96},{32,64},{64,32},{96,0},{1,97},{33,65},{65,33},{97,1},{2,98}... | collective-permute-start | bytes 196616 | tf_op jit(solution)/shard_map/ppermute | solution.py:428
  47.4 8.7 %collective-permute-start.1 = (bf16[2,32,512]{2,1,0:T(8,128)(2,1)S(1)}, bf16[2,32,512]{2,1,0:T(8,128)(2,1)S(1)}, u32[]{:S(2)}, u32[]{:S(2)}) collective-permute-start(bf16[2,32,512]{2,1,0:T(8,128)(2,1)S(1)} %bitcast.3), channel_id=1, source_target_pairs={{0,64},{32,96},{64,0},{96,32},{1,65},{33,97},{65,1},{97,33},{2,66}... | collective-permute-start | bytes 196616 | tf_op jit(solution)/shard_map/ppermute | solution.py:428
  47.9 8.1 %collective-permute-start = (bf16[2,32,512]{2,1,0:T(8,128)(2,1)S(1)}, bf16[2,32,512]{2,1,0:T(8,128)(2,1)S(1)}, u32[]{:S(2)}, u32[]{:S(2)}) collective-permute-start(bf16[2,32,512]{2,1,0:T(8,128)(2,1)S(1)} %bitcast.4), channel_id=1, source_target_pairs={{0,32},{32,0},{64,96},{96,64},{1,33},{33,1},{65,97},{97,65},{2,34}... | collective-permute-start | bytes 196616 | tf_op jit(solution)/shard_map/ppermute | solution.py:428

commit v4 on v3

--- a/solution.py
+++ b/solution.py
@@ -27,6 +27,7 @@
 SIZES = (8, 8, 8, 8)
 STARTS = tuple(sum(SIZES[:n]) for n in range(len(SIZES)))
 ALL = ("dp", "slab")
+BACK = 10
 BF = jnp.bfloat16
 F32 = jnp.float32
 VMEM_LIMIT = 56 << 20
@@ -106,7 +107,8 @@
 
 
 def twice_gelu_slope(x):
-    bell = jnp.exp2(x * x * (-0.5 * math.log2(math.e)) + math.log2(2.0 * 0.3989422804014327))
+    u = x * math.sqrt(0.5 * math.log2(math.e))
+    bell = jnp.exp2(math.log2(2.0 * 0.3989422804014327) - u * u)
     return 1.0 + (lax.erf(x * 0.7071067811865476) + x * bell)
 
 
@@ -248,7 +250,7 @@
     )(w_local, grad_out, pre_act)
 
 
-def mix_kernel(got_ref, wf_ref, wi_ref, send_ref, rows_ref, v_ref, out_ref, g_ref, back_ref):
+def mix_kernel(got_ref, wf_ref, wi_ref, send_hbm, rows_ref, v_ref, out_ref, g_ref, back_ref, send_ref, out_sem):
     rows_ref[...] = got_ref[...].astype(F32).reshape(DEVS * 24, 128)
     for j in range(4):
         for og in range(NB):
@@ -267,13 +269,13 @@
         grad = grad + dot(left, wf_ref[ql])
     g_ref[...] = grad
 
-    turned = grad.T
-    for r in range(2):
-        for ql in range(QL):
-            at = (r * QL + ql) * KX
-            for og in range(NB):
-                first = og * NS * 16 + 8 + r * QL + ql
-                out_ref[pl.ds(first, KX, stride=16), :] = turned[at : at + KX]
+    for og in range(NB):
+        own = [grad[b * C + og * SHARE : b * C + (og + 1) * SHARE] for b in range(NB)]
+        own = jnp.concatenate(own, 0)
+        for r in range(2):
+            part = [own[:, (r * QL + ql) * KX : (r * QL + ql + 1) * KX] for ql in range(QL)]
+            turned = jnp.concatenate(part, 0).T
+            out_ref[pl.ds(og * NS * BACK + 8 + r, KX, stride=BACK), :] = turned
 
     for ig in range(4):
         acc = [[jnp.zeros((8, 128), F32) for _ in range(2)] for _ in range(NB)]
@@ -291,23 +293,33 @@
 
     back = back_ref[...].astype(BF)
     outs = [dot(back, wi_ref[ql]) for ql in range(QL)]
+    copies = []
     for b in range(NB):
         turned = jnp.concatenate([outs[ql][b * C : (b + 1) * C] for ql in range(QL)], 0).T
         for s in range(NS):
-            out_ref[pl.ds((b * NS + s) * 16, 8), :] = turned[s * 8 : s * 8 + 8]
-    send_ref[...] = out_ref[...].reshape(DEVS, 16, 128).astype(BF)
+            out_ref[pl.ds((b * NS + s) * BACK, 8), :] = turned[s * 8 : s * 8 + 8]
+        part = pl.ds(b * NS * BACK, NS * BACK)
+        send_ref[part] = out_ref[part, :].astype(BF)
+        copies.append(pltpu.make_async_copy(send_ref.at[part], send_hbm.at[part], out_sem.at[b]))
+        copies[-1].start()
+    for copy in copies:
+        copy.wait()
 
 
 def mix(got):
     return pl.pallas_call(
         mix_kernel,
-        out_shape=jax.ShapeDtypeStruct((DEVS, 16, 128), BF),
+        in_specs=[pl.BlockSpec(memory_space=pltpu.VMEM)] * 3,
+        out_specs=pl.BlockSpec(memory_space=pl.ANY),
+        out_shape=jax.ShapeDtypeStruct((DEVS * BACK, 128), BF),
         scratch_shapes=[
             pltpu.VMEM((DEVS * 24, 128), F32),
             pltpu.VMEM((16 * 128, 128), F32),
-            pltpu.VMEM((DEVS * 16, 128), F32),
+            pltpu.VMEM((DEVS * BACK, 128), F32),
             pltpu.VMEM((128, 256), F32),
             pltpu.VMEM((128, 256), F32),
+            pltpu.VMEM((DEVS * BACK, 128), BF),
+            pltpu.SemaphoreType.DMA((NB,)),
         ],
         compiler_params=pltpu.CompilerParams(vmem_limit_bytes=16 << 20),
         name="mix",
@@ -331,18 +343,18 @@
 
     for n in range(STEPS):
         fetch(n).start()
-    rows_ref[...] = got_ref[...].astype(F32).reshape(DEVS * 16, 128)
+    rows_ref[...] = got_ref[...].astype(F32)
     for qh in range(KY // QL):
-        group = [rows_ref[pl.ds((qh * KZ + kz) * 16, 8), :] for kz in range(KZ)]
+        group = [rows_ref[pl.ds((qh * KZ + kz) * BACK, 8), :] for kz in range(KZ)]
         turned = jnp.concatenate(group, 0).T
         for ql in range(QL):
             x_ref[pl.ds(qh * QL + ql, C, stride=KY), :] = turned[ql * C : (ql + 1) * C]
     for r in range(2):
         for tile in range(4):
             group = []
-            for q in range(2 * QL):
-                first = (tile * 2 + q // QL) * KZ * 16 + 8 + r * QL + q % QL
-                group.append(rows_ref[pl.ds(first, KZ, stride=16), :])
+            for qh in range(tile * 2, tile * 2 + 2):
+                row = rows_ref[pl.ds(qh * KZ * BACK + 8 + r, KZ, stride=BACK), :]
+                group += [row[:, ql * 32 : (ql + 1) * 32] for ql in range(QL)]
             g_ref[r, :, tile * 128 : (tile + 1) * 128] = jnp.concatenate(group, 0).T
     for hop, fm in enumerate((fm0, fm1, fm2, fm3)):
         u_ref[hop] = fm[...].astype(F32)
@@ -373,7 +385,7 @@
             i = step * CB + k
             wr, wi = jnp.zeros((SHARE, KY * KZ), F32), jnp.zeros((SHARE, KY * KZ), F32)
             for hop in range(NB):
-                at = pl.multiple_of((me ^ hop) * C + me * SHARE, SHARE)
+                at = pl.multiple_of((me ^ hop) * SHARE, SHARE)
                 gr, gi = g_ref[0, pl.ds(at, SHARE), :], g_ref[1, pl.ds(at, SHARE), :]
                 ur, ui = u_ref[hop, 0, pl.ds(i, 1), :], u_ref[hop, 1, pl.ds(i, 1), :]
                 wr = wr + gr * ur + gi * ui
@@ -400,9 +412,9 @@
             jax.ShapeDtypeStruct((1, 2, C, SHARE, KY * KZ), F32),
         ],
         scratch_shapes=[
-            pltpu.VMEM((DEVS * 16, 128), F32),
+            pltpu.VMEM((DEVS * BACK, 128), F32),
             pltpu.VMEM((C * KY, 128), F32),
-            pltpu.VMEM((2, 128, KY * KZ), F32),
+            pltpu.VMEM((2, NB * SHARE, KY * KZ), F32),
             pltpu.VMEM((NB, 2, C, KY * KZ), F32),
             pltpu.VMEM((C, NY, 256), BF),
             pltpu.VMEM((C, NP, NY, NZ), BF),
@@ -426,8 +438,9 @@
     got, local = lax.optimization_barrier((got, local))
     fm = forward_modes.reshape(2, C, KY * KZ)
     fms = [fm] + [lax.ppermute(fm, "dp", [(b, b ^ hop) for b in range(NB)]) for hop in range(1, NB)]
-    got = lax.all_to_all(mix(got), ALL, 0, 0, tiled=True)
-    return synthesis(me.reshape(1), got, local, fms)
+    back = mix(got).reshape(DEVS, BACK // 2, 2, 128)
+    back = lax.all_to_all(back, ALL, 0, 0, tiled=True).reshape(DEVS * BACK, 128)
+    return synthesis(me.reshape(1), back, local, fms)
 
 
 def solution(mesh):

time: 63.5 us -> 62.2 us (0.980)
  waiting for transfers between devices: 18.2 us -> 16.1 us
  Pallas kernels: 24.8 us -> 25.7 us
    ppermute x3, waiting for transfers between devices: 7.99 us -> 5.97 us  [shards(): lax.ppermute(fm, 'dp', [(b, b ^ hop) for b in range(NB)])]
    pallas_call x1, Pallas kernels: 4.74 us -> 5.56 us  [synthesis(): pl.pallas_call(synthesis_kernel, in_specs=[pl.BlockSpec(memory_space=pltp...]
  transfers between devices with their start and end apart: 5 -> 5, of which waited for: 3 -> 4; matrix products, arithmetic and copies ran while one was open for 0% -> 0% of each run, Pallas kernels for 14% -> 14%
where the time goes in v4:
time: 62.2 us; the launch traced here: 61.9 us
  Pallas kernels  25.7 us (41%)
  starting transfers between devices  19.3 us (31%)
  waiting for transfers between devices  16.1 us (26%)
  between operations  0.72 us (1%)
    all_to_all x1, starting transfers between devices, shards(): got = lax.all_to_all(send, ALL, 0, 0, tiled=True)  11.5 us
    pallas_call x1, Pallas kernels, analysis(): pl.pallas_call(analysis_kernel, in_specs=[hbm, hbm, hbm, hbm, vmem], out_...  9.01 us
    pallas_call x1, Pallas kernels, local_map(): pl.pallas_call(local_kernel, grid=(NY // YB,), in_specs=[pl.BlockSpec((C,...  8.57 us
    all_to_all x1, waiting for transfers between devices, shards(): got = lax.all_to_all(send, ALL, 0, 0, tiled=True)  7.91 us
    ppermute x3, waiting for transfers between devices, shards(): lax.ppermute(fm, 'dp', [(b, b ^ hop) for b in range(NB)])  5.97 us
    pallas_call x1, Pallas kernels, synthesis(): pl.pallas_call(synthesis_kernel, in_specs=[pl.BlockSpec(memory_space=pltp...  5.56 us
    all_to_all x1, starting transfers between devices, shards(): back = lax.all_to_all(back, ALL, 0, 0, tiled=True).reshape(DEVS * BACK, 128)  4.43 us
    ppermute x3, starting transfers between devices, shards(): lax.ppermute(fm, 'dp', [(b, b ^ hop) for b in range(NB)])  3.41 us
  transfers between devices with their start and end apart: 5, of which 4 were waited for; matrix products, arithmetic and copies ran while one was open for 0% of the time, Pallas kernels for 14%

profile of v4, /device:TPU:1, one launch (start us, length us, event | category | flops | bytes accessed | tf_op | source)
XLA Modules:
  0.0 61.9 jit_solution(1642552421249049474)
XLA Ops:
  0.6 9.0 %analysis.1 = bf16[128,24,128]{2,1,0:T(8,128)(2,1)} custom-call(bf16[1,32,4,128,128]{4,3,2,1,0:T(8,128)(2,1)} %go_ref, bf16[1,32,4,128,128]{4,3,2,1,0:T(8,128)(2,1)} %pa_ref, bf16[1,2,32,8,512]{4,3,2,1,0:T(8,128)(2,1)} %sw_hbm.1, bf16[512,256]{1,0:T(8,128)(2,1)} %constant.28.za_hbm, bf16[64,128]{1,0:T(8,128)(2,1)} %constant.29.cs_ref), custom_call_target="tpu_custom_call" | custom-call | tf_op jit(solution)/shard_map/analysis/pallas_call | solution.py:191
  9.6 11.5 %all-to-all-start = ((bf16[128,24,128]{2,1,0:T(8,128)(2,1)}), bf16[128,24,128]{2,1,0:T(8,128)(2,1)S(1)}, u32[]{:S(2)}, u32[]{:S(2)}) async-start(bf16[128,24,128]{2,1,0:T(8,128)(2,1)} %analysis.1), calls=%async_computation | async-start | bytes 1572864 | tf_op jit(solution)/shard_map/all_to_all | solution.py:436
  21.2 0.0 copy-start
  21.2 0.0 copy-start.1
  21.2 0.0 copy-start.3
  21.2 0.0 copy-start.2
  21.2 0.0 copy-start.4
  21.2 8.6 %local_map.1.local_hbm = bf16[32,4,128,128]{3,2,1,0:T(8,128)(2,1)} custom-call(bf16[32,32]{1,0:T(8,128)(2,1)} %w_ref.1, bf16[1,32,4,128,128]{4,3,2,1,0:T(8,128)(2,1)} %go_ref, bf16[1,32,4,128,128]{4,3,2,1,0:T(8,128)(2,1)} %pa_ref), custom_call_target="tpu_custom_call" | custom-call | flops 1073741824 | bytes 12582912 | tf_op jit(solution)/shard_map/local_map/pallas_call | solution.py:240
  29.8 7.9 %all-to-all-done.got_ref = bf16[128,24,128]{2,1,0:T(8,128)(2,1)S(1)} async-done(((bf16[128,24,128]{2,1,0:T(8,128)(2,1)}), bf16[128,24,128]{2,1,0:T(8,128)(2,1)S(1)}, u32[]{:S(2)}, u32[]{:S(2)}) %all-to-all-start) | async-done | bytes 786464 | tf_op jit(solution)/shard_map/all_to_all | solution.py:436
  37.7 0.0 copy-done
  37.7 0.0 copy-done.1
  37.7 2.6 %mix.1 = bf16[1280,128]{1,0:T(8,128)(2,1)} custom-call(bf16[128,24,128]{2,1,0:T(8,128)(2,1)S(1)} %all-to-all-done.got_ref, bf16[4,256,256]{2,1,0:T(8,128)(2,1)S(1)} %copy-done.1, bf16[4,256,256]{2,1,0:T(8,128)(2,1)S(1)} %copy-done), custom_call_target="tpu_custom_call" | custom-call | tf_op jit(solution)/shard_map/mix/pallas_call | solution.py:310
  40.3 4.4 %all-to-all-start.1 = ((bf16[128,5,2,128]{3,2,1,0:T(2,128)(2,1)}), bf16[128,5,2,128]{3,2,1,0:T(2,128)(2,1)S(1)}, u32[]{:S(2)}, u32[]{:S(2)}) async-start(bf16[128,5,2,128]{3,2,1,0:T(2,128)(2,1)} %bitcast.1), calls=%async_computation.1 | async-start | bytes 655360 | tf_op jit(solution)/shard_map/all_to_all | solution.py:442
  44.7 0.0 copy-done.3
  44.7 2.7 %collective-permute-start.2 = (bf16[2,32,512]{2,1,0:T(8,128)(2,1)S(1)}, bf16[2,32,512]{2,1,0:T(8,128)(2,1)S(1)}, u32[]{:S(2)}, u32[]{:S(2)}) collective-permute-start(bf16[2,32,512]{2,1,0:T(8,128)(2,1)S(1)} %bitcast.5), channel_id=1, source_target_pairs={{0,96},{32,64},{64,32},{96,0},{1,97},{33,65},{65,33},{97,1},{2,98}... | collective-permute-start | bytes 196616 | tf_op jit(solution)/shard_map/ppermute | solution.py:440
  47.5 0.5 collective-permute-start.1
  48.0 0.2 collective-permute-start
  48.2 4.1 %collective-permute-done.2.fm3 = bf16[2,32,512]{2,1,0:T(8,128)(2,1)S(1)} collective-permute-done((bf16[2,32,512]{2,1,0:T(8,128)(2,1)S(1)}, bf16[2,32,512]{2,1,0:T(8,128)(2,1)S(1)}, u32[]{:S(2)}, u32[]{:S(2)}) %collective-permute-start.2) | collective-permute-done | bytes 65568 | tf_op jit(solution)/shard_map/ppermute | solution.py:440
  52.3 1.9 %collective-permute-done.1.fm2 = bf16[2,32,512]{2,1,0:T(8,128)(2,1)S(1)} collective-permute-done((bf16[2,32,512]{2,1,0:T(8,128)(2,1)S(1)}, bf16[2,32,512]{2,1,0:T(8,128)(2,1)S(1)}, u32[]{:S(2)}, u32[]{:S(2)}) %collective-permute-start.1) | collective-permute-done | bytes 65568 | tf_op jit(solution)/shard_map/ppermute | solution.py:440
  54.1 0.0 collective-permute-done.fm1
  54.1 2.2 %all-to-all-done.1 = bf16[128,5,2,128]{3,2,1,0:T(2,128)(2,1)S(1)} async-done(((bf16[128,5,2,128]{3,2,1,0:T(2,128)(2,1)}), bf16[128,5,2,128]{3,2,1,0:T(2,128)(2,1)S(1)}, u32[]{:S(2)}, u32[]{:S(2)}) %all-to-all-start.1) | async-done | bytes 327712 | tf_op jit(solution)/shard_map/all_to_all | solution.py:442
  56.4 0.0 copy-done.2
  56.4 0.0 copy-done.4
  56.4 5.6 %synthesis.1 = (bf16[1,32,4,128,128]{4,3,2,1,0:T(8,128)(2,1)}, f32[1,2,32,8,512]{4,3,2,1,0:T(8,128)}) custom-call(s32[1]{0:T(128)} %bitcast.me_ref, bf16[1280,128]{1,0:T(8,128)(2,1)S(1)} %bitcast.4, bf16[32,4,128,128]{3,2,1,0:T(8,128)(2,1)} %local_map.1.local_hbm, bf16[2,32,512]{2,1,0:T(8,128)(2,1)S(1)} %bitcast.8, ...), custom_call_target="tpu_custom_call" | custom-call | tf_op jit(solution)/shard_map/synthesis/pallas_call | solution.py:406
Async XLA Ops:
  9.6 28.1 %all-to-all-start = ((bf16[128,24,128]{2,1,0:T(8,128)(2,1)}), bf16[128,24,128]{2,1,0:T(8,128)(2,1)S(1)}, u32[]{:S(2)}, u32[]{:S(2)}) async-start(bf16[128,24,128]{2,1,0:T(8,128)(2,1)} %analysis.1), calls=%async_computation | async-start | bytes 1572864 | tf_op jit(solution)/shard_map/all_to_all | solution.py:436
  21.2 16.5 %copy-start = (bf16[4,256,256]{2,1,0:T(8,128)(2,1)S(1)}, bf16[4,256,256]{2,1,0:T(8,128)(2,1)}, u32[]{:S(2)}) copy-start(bf16[4,256,256]{2,1,0:T(8,128)(2,1)} %constant.31.wi_ref) | copy-start | bytes 1572868
  21.2 16.5 %copy-start.1 = (bf16[4,256,256]{2,1,0:T(8,128)(2,1)S(1)}, bf16[4,256,256]{2,1,0:T(8,128)(2,1)}, u32[]{:S(2)}) copy-start(bf16[4,256,256]{2,1,0:T(8,128)(2,1)} %constant.30.wf_ref) | copy-start | bytes 1572868
  21.2 23.5 %copy-start.3 = (bf16[1,1,2,32,512]{4,3,2,1,0:T(8,128)(2,1)S(1)}, bf16[1,1,2,32,512]{4,3,2,1,0:T(8,128)(2,1)}, u32[]{:S(2)}) copy-start(bf16[1,1,2,32,512]{4,3,2,1,0:T(8,128)(2,1)} %param.13) | copy-start | bytes 196612
  21.2 35.2 %copy-start.2 = (bf16[256,512]{1,0:T(8,128)(2,1)S(1)}, bf16[256,512]{1,0:T(8,128)(2,1)}, u32[]{:S(2)}) copy-start(bf16[256,512]{1,0:T(8,128)(2,1)} %constant.33.zs_ref) | copy-start | bytes 786436
  21.2 35.2 %copy-start.4 = (bf16[256,32]{1,0:T(8,128)(2,1)S(1)}, bf16[256,32]{1,0:T(8,128)(2,1)}, u32[]{:S(2)}) copy-start(bf16[256,32]{1,0:T(8,128)(2,1)} %constant.32.cs_ref) | copy-start | bytes 49156
  40.3 16.1 %all-to-all-start.1 = ((bf16[128,5,2,128]{3,2,1,0:T(2,128)(2,1)}), bf16[128,5,2,128]{3,2,1,0:T(2,128)(2,1)S(1)}, u32[]{:S(2)}, u32[]{:S(2)}) async-start(bf16[128,5,2,128]{3,2,1,0:T(2,128)(2,1)} %bitcast.1), calls=%async_computation.1 | async-start | bytes 655360 | tf_op jit(solution)/shard_map/all_to_all | solution.py:442
  44.7 7.5 %collective-permute-start.2 = (bf16[2,32,512]{2,1,0:T(8,128)(2,1)S(1)}, bf16[2,32,512]{2,1,0:T(8,128)(2,1)S(1)}, u32[]{:S(2)}, u32[]{:S(2)}) collective-permute-start(bf16[2,32,512]{2,1,0:T(8,128)(2,1)S(1)} %bitcast.5), channel_id=1, source_target_pairs={{0,96},{32,64},{64,32},{96,0},{1,97},{33,65},{65,33},{97,1},{2,98}... | collective-permute-start | bytes 196616 | tf_op jit(solution)/shard_map/ppermute | solution.py:440
  47.5 6.6 %collective-permute-start.1 = (bf16[2,32,512]{2,1,0:T(8,128)(2,1)S(1)}, bf16[2,32,512]{2,1,0:T(8,128)(2,1)S(1)}, u32[]{:S(2)}, u32[]{:S(2)}) collective-permute-start(bf16[2,32,512]{2,1,0:T(8,128)(2,1)S(1)} %bitcast.6), channel_id=1, source_target_pairs={{0,64},{32,96},{64,0},{96,32},{1,65},{33,97},{65,1},{97,33},{2,66}... | collective-permute-start | bytes 196616 | tf_op jit(solution)/shard_map/ppermute | solution.py:440
  48.0 6.1 %collective-permute-start = (bf16[2,32,512]{2,1,0:T(8,128)(2,1)S(1)}, bf16[2,32,512]{2,1,0:T(8,128)(2,1)S(1)}, u32[]{:S(2)}, u32[]{:S(2)}) collective-permute-start(bf16[2,32,512]{2,1,0:T(8,128)(2,1)S(1)} %bitcast.7), channel_id=1, source_target_pairs={{0,32},{32,0},{64,96},{96,64},{1,33},{33,1},{65,97},{97,65},{2,34}... | collective-permute-start | bytes 196616 | tf_op jit(solution)/shard_map/ppermute | solution.py:440
